TPU v7x, 32 devices: a whole 2x2x4 slice. The times are simulated.
32 devices in a mesh: parts: 2 (over y), tm: 4 (over z), chan: 4 (over x, core).
Axes of the slice: x: 2, y: 2, z: 4, core: 2. Of those that a mesh axis runs over, the one named last changes fastest.
Arguments:
- records: float32 [512, 1024], P(('parts', 'chan'), 'tm'), parts along dimension 0, may hold values from -8 to 8
- fir_taps: float32 [129], replicated, may hold values from -0.5 to 0.5
- matchings: int32 [2, 4], replicated, may hold values from 0 to 3, as said below
Outputs:
- correlograms: bfloat16 [2, 8, 64, 16448], P(None, ('parts', 'chan'), 'tm'), parts along dimension 1
There are 2 independent parts, one for each index of `parts`. A program takes and returns all parts, laid end to end along the dimension named above; an argument that names none is the same for every part. Nothing has to cross between parts.
Inputs may be any that keep to these rules, and one draw needn't show every extreme that they name: `matchings`: each row sends every group to another group, and following a row from any group visits all 4 groups in one cycle.
All inputs are finite; a program needn't handle non-finite values.
Results may differ from a plain program's by a relative error of at most 0.0049.
Values may be sent and summed in bfloat16 or wider, within the bound.
No kernel may reach another device: no remote copies, remote signals or barrier semaphores. Data moves between devices by JAX's collectives and lax.ppermute only.
A program may use at most 64 MiB of HBM per device.

v0:
```python
import math

import jax
import jax.numpy as jnp
from jax import lax
from jax.sharding import PartitionSpec as P

AVG = 65
MAXLAG = 128
LAGS = 257


EPSILON = 1e-05


def extended_2(cells, sides, width):
    for axis, dim in sides:
        count = lax.axis_size(axis)
        ends = count - 1
        head = lax.slice_in_dim(cells, 0, width, axis=dim)
        tail = lax.slice_in_dim(cells, cells.shape[dim] - width, cells.shape[dim], axis=dim)
        cells = jnp.concatenate(
            [
                lax.ppermute(tail, axis, [(i, (i + 1) % count) for i in range(ends)]),
                cells,
                lax.ppermute(head, axis, [((i + 1) % count, i) for i in range(ends)]),
            ],
            axis=dim,
        )
    return cells


def falling(window, row_count):
    leading = window.shape[:-1]
    extended = jnp.concatenate([window, jnp.zeros(leading + (1,), window.dtype)], axis=-1)
    span_width = extended.shape[-1]
    repeated = jnp.broadcast_to(extended[..., None, :], leading + (row_count, span_width))
    repeated = repeated.reshape(leading + (row_count * span_width,))[
        ..., : row_count * (span_width - 1)
    ]
    return repeated.reshape(leading + (row_count, span_width - 1))[..., row_count - 1 :]


def fir_matrix(fir_taps, row_count, col_count):
    tap_count = fir_taps.shape[0]
    padded = jnp.concatenate(
        [
            jnp.zeros((row_count - tap_count,), jnp.float32),
            fir_taps,
            jnp.zeros((col_count - 1,), jnp.float32),
        ]
    )
    return falling(padded, row_count)


def normalize(records, fir_taps):
    tap_half = fir_taps.shape[0] // 2
    avg_half = AVG // 2
    samples_dev = records.shape[1]
    widened = extended_2(records, (("tm", 1),), tap_half + avg_half)
    filtered = jnp.dot(
        widened,
        fir_matrix(fir_taps, samples_dev + 2 * (tap_half + avg_half), samples_dev + 2 * avg_half),
        precision=lax.Precision.HIGHEST,
        preferred_element_type=jnp.float32,
    )
    global_time = (
        lax.axis_index("tm") * samples_dev
        - avg_half
        + lax.iota(jnp.int32, samples_dev + 2 * avg_half)
    )
    inside = (global_time >= 0) & (global_time < samples_dev * lax.axis_size("tm"))
    filtered = jnp.where(inside[None, :], filtered, 0.0)
    magnitude = jnp.abs(filtered)
    rows_at = lax.broadcasted_iota(jnp.int32, (samples_dev + 2 * avg_half, samples_dev), 0)
    cols_at = lax.broadcasted_iota(jnp.int32, (samples_dev + 2 * avg_half, samples_dev), 1)
    band_matrix = ((rows_at >= cols_at) & (rows_at <= cols_at + 2 * avg_half)).astype(jnp.float32)
    local_mean = (
        jnp.dot(
            magnitude,
            band_matrix,
            precision=lax.Precision.HIGHEST,
            preferred_element_type=jnp.float32,
        )
        / AVG
    )
    centre = filtered[:, avg_half : avg_half + samples_dev]
    return (centre / (local_mean + EPSILON)).astype(jnp.bfloat16)


def local(records, fir_taps, matchings):
    normed = normalize(records, fir_taps)
    group_ch, samples_dev = normed.shape
    group_count = lax.axis_size("chan")
    group_index = lax.axis_index("chan")
    match_count = matchings.shape[0]
    every_group = lax.all_gather(normed, "chan", axis=0, tiled=True).reshape(
        group_count, group_ch, samples_dev
    )
    partners = jnp.take(every_group, matchings[:, group_index], axis=0)
    time_count = lax.axis_size("tm")
    scaling = 1.0 / math.sqrt(samples_dev * time_count)
    row_share = group_ch // time_count
    own_rows = lax.all_to_all(normed, "tm", split_axis=0, concat_axis=1, tiled=True)
    padded = jnp.pad(own_rows, ((0, 0), (MAXLAG, MAXLAG)))
    initial = jnp.zeros((match_count, row_share, LAGS, group_ch), jnp.float32)
    incoming = lax.all_gather(partners, "tm", axis=2, tiled=True)
    part_width = incoming.shape[2]
    block_width = math.gcd(part_width, 128)
    block_count = part_width // block_width

    def one_block(block_index, running):
        offset = block_index * block_width
        window = lax.dynamic_slice_in_dim(padded, offset, block_width + 2 * MAXLAG, 1)
        lagged = falling(window, LAGS)
        piece = lax.dynamic_slice_in_dim(incoming, offset, block_width, 2)
        return running + jnp.einsum(
            "ilt,mjt->milj", lagged, piece, preferred_element_type=jnp.float32
        )

    summed = lax.fori_loop(0, block_count, one_block, initial)
    result = (
        (summed * scaling).astype(jnp.bfloat16).reshape(match_count, 1, row_share, LAGS * group_ch)
    )
    return result


def solution(mesh):
    in_specs = (P(("parts", "chan"), "tm"), P(), P())
    out_specs = P(None, ("parts", "chan"), "tm", None)
    return jax.shard_map(local, mesh=mesh, in_specs=in_specs, out_specs=out_specs, check_vma=False)
```

profile of v0, /device:TPU:0, one launch (start us, length us, event | category | flops | bytes accessed | tf_op | source)
XLA Modules:
  0.0 187.4 jit_solution(5128259698536419068)
XLA Ops:
  0.8 4.9 %collective-permute-start = (f32[64,96]{1,0:T(8,128)S(1)}, f32[64,96]{1,0:T(8,128)S(1)}, u32[]{:S(2)}, u32[]{:S(2)}) collective-permute-start(f32[64,96]{1,0:T(8,128)S(1)} %get-tuple-element.108), channel_id=1, source_target_pairs={{0,4},{4,8},{8,12},{1,5},{5,9},{9,13},{2,6},{6,10},{10,14},{3,7},{... | collective-permute-start | bytes 73736 | tf_op jit(solution)/shard_map/ppermute | solution.py:24
  13.2 5.6 %all_gather.6 = bf16[256,256]{1,0:T(8,128)(2,1)S(1)} all-gather(bf16[64,256]{1,0:T(8,128)(2,1)} %fusion.14), channel_id=1, replica_groups=mesh['parts'=2,'tm'=4,'chan'=4] {'chan'}, dimensions={0}, use_global_device_ids=true | all-gather | bytes 163840 | tf_op jit(solution)/shard_map/all_gather | solution.py:97
  18.8 4.9 %all-to-all-start = ((bf16[4,16,256]{2,1,0:T(8,128)(2,1)}), bf16[4,16,256]{2,1,0:T(8,128)(2,1)S(1)}, u32[]{:S(2)}, u32[]{:S(2)}) async-start(bf16[4,16,256]{2,1,0:T(8,128)(2,1)} %bitcast.1), calls=%async_computation | async-start | bytes 65536 | tf_op jit(solution)/shard_map/all_to_all | solution.py:104
  24.3 14.4 %all_gather.7 = bf16[2,64,1024]{2,1,0:T(8,128)(2,1)S(1)} all-gather(bf16[2,64,256]{2,1,0:T(8,128)(2,1)S(1)} %broadcast_select_fusion), channel_id=1, replica_groups=mesh['parts'=2,'tm'=4,'chan'=4] {'tm'}, dimensions={2}, use_global_device_ids=true | all-gather | bytes 327680 | tf_op jit(solution)/shard_map/all_gather | solution.py:107
  38.8 140.0 %while.14 = (s32[]{:T(128)}, f32[2,16,257,64]{2,3,1,0:T(8,128)}, bf16[2,64,1024]{2,1,0:T(8,128)(2,1)S(1)}, bf16[16,1280]{1,0:T(8,128)(2,1)S(1)}, s32[]{:T(128)},...) while((s32[]{:T(128)}, f32[2,16,257,64]{2,3,1,0:T(8,128)}, ...), condition=%wide.region_1.2_spmd.clone, body=%wide.region_0.1_spmd.clone.sunk | while | flops 135794688 | bytes 27517284 | solution.py:121
  41.1 6.5 %reshape.62 = bf16[16,98945]{1,0:T(8,128)(2,1)S(1)} reshape(bf16[16,257,385]{2,1,0:T(8,128)(2,1)} %broadcast_in_dim.60) | data formatting | bytes 6332480 | tf_op jit(solution)/shard_map/while/body/eval_jaxpr/reshape | solution.py:38
  57.0 6.5 %reshape.62 = bf16[16,98945]{1,0:T(8,128)(2,1)S(1)} reshape(bf16[16,257,385]{2,1,0:T(8,128)(2,1)} %broadcast_in_dim.60) | data formatting | bytes 6332480 | tf_op jit(solution)/shard_map/while/body/eval_jaxpr/reshape | solution.py:38
  68.3 4.2 %bitcast_add_fusion.2 = f32[2,16,257,64]{2,3,1,0:T(8,128)} fusion(f32[2,16,257,64]{2,3,1,0:T(8,128)} %get-tuple-element.146, pred[]{:T(512)S(6)} %compare.5, bf16[16,257,384]{2,1,0:T(8,128)(2,1)S(1)} %reshape.63, bf16[2,64,1024]{2,1,0:T(8,128)(2,1)S(1)} %get-tuple-element.157, s32[]{:T(128)S(6)} %select_n.48), kind=kOutput, calls=%fused_computation.1.clone.1 | convolution fusion | flops 135794688 | bytes 5324805 | tf_op jit(solution)/shard_map/while/body/eval_jaxpr/ilt,mjt->milj/dot_general | solution.py:117
  74.7 6.5 %reshape.62 = bf16[16,98945]{1,0:T(8,128)(2,1)S(1)} reshape(bf16[16,257,385]{2,1,0:T(8,128)(2,1)} %broadcast_in_dim.60) | data formatting | bytes 6332480 | tf_op jit(solution)/shard_map/while/body/eval_jaxpr/reshape | solution.py:38
  83.1 2.9 %reshape.63 = bf16[16,257,384]{2,1,0:T(8,128)(2,1)S(1)} reshape(bf16[16,98688]{1,0:T(8,128)(2,1)} %slice.55) | data formatting | bytes 6316032 | tf_op jit(solution)/shard_map/while/body/eval_jaxpr/reshape | solution.py:41
  86.0 4.1 %bitcast_add_fusion.2 = f32[2,16,257,64]{2,3,1,0:T(8,128)} fusion(f32[2,16,257,64]{2,3,1,0:T(8,128)} %get-tuple-element.146, pred[]{:T(512)S(6)} %compare.5, bf16[16,257,384]{2,1,0:T(8,128)(2,1)S(1)} %reshape.63, bf16[2,64,1024]{2,1,0:T(8,128)(2,1)S(1)} %get-tuple-element.157, s32[]{:T(128)S(6)} %select_n.48), kind=kOutput, calls=%fused_computation.1.clone.1 | convolution fusion | flops 135794688 | bytes 5324805 | tf_op jit(solution)/shard_map/while/body/eval_jaxpr/ilt,mjt->milj/dot_general | solution.py:117
  92.4 6.5 %reshape.62 = bf16[16,98945]{1,0:T(8,128)(2,1)S(1)} reshape(bf16[16,257,385]{2,1,0:T(8,128)(2,1)} %broadcast_in_dim.60) | data formatting | bytes 6332480 | tf_op jit(solution)/shard_map/while/body/eval_jaxpr/reshape | solution.py:38
  103.7 4.1 %bitcast_add_fusion.2 = f32[2,16,257,64]{2,3,1,0:T(8,128)} fusion(f32[2,16,257,64]{2,3,1,0:T(8,128)} %get-tuple-element.146, pred[]{:T(512)S(6)} %compare.5, bf16[16,257,384]{2,1,0:T(8,128)(2,1)S(1)} %reshape.63, bf16[2,64,1024]{2,1,0:T(8,128)(2,1)S(1)} %get-tuple-element.157, s32[]{:T(128)S(6)} %select_n.48), kind=kOutput, calls=%fused_computation.1.clone.1 | convolution fusion | flops 135794688 | bytes 5324805 | tf_op jit(solution)/shard_map/while/body/eval_jaxpr/ilt,mjt->milj/dot_general | solution.py:117
  110.2 6.5 %reshape.62 = bf16[16,98945]{1,0:T(8,128)(2,1)S(1)} reshape(bf16[16,257,385]{2,1,0:T(8,128)(2,1)} %broadcast_in_dim.60) | data formatting | bytes 6332480 | tf_op jit(solution)/shard_map/while/body/eval_jaxpr/reshape | solution.py:38
  121.5 4.2 %bitcast_add_fusion.2 = f32[2,16,257,64]{2,3,1,0:T(8,128)} fusion(f32[2,16,257,64]{2,3,1,0:T(8,128)} %get-tuple-element.146, pred[]{:T(512)S(6)} %compare.5, bf16[16,257,384]{2,1,0:T(8,128)(2,1)S(1)} %reshape.63, bf16[2,64,1024]{2,1,0:T(8,128)(2,1)S(1)} %get-tuple-element.157, s32[]{:T(128)S(6)} %select_n.48), kind=kOutput, calls=%fused_computation.1.clone.1 | convolution fusion | flops 135794688 | bytes 5324805 | tf_op jit(solution)/shard_map/while/body/eval_jaxpr/ilt,mjt->milj/dot_general | solution.py:117
  127.9 6.5 %reshape.62 = bf16[16,98945]{1,0:T(8,128)(2,1)S(1)} reshape(bf16[16,257,385]{2,1,0:T(8,128)(2,1)} %broadcast_in_dim.60) | data formatting | bytes 6332480 | tf_op jit(solution)/shard_map/while/body/eval_jaxpr/reshape | solution.py:38
  136.3 2.9 %reshape.63 = bf16[16,257,384]{2,1,0:T(8,128)(2,1)S(1)} reshape(bf16[16,98688]{1,0:T(8,128)(2,1)} %slice.55) | data formatting | bytes 6316032 | tf_op jit(solution)/shard_map/while/body/eval_jaxpr/reshape | solution.py:41
  139.2 4.1 %bitcast_add_fusion.2 = f32[2,16,257,64]{2,3,1,0:T(8,128)} fusion(f32[2,16,257,64]{2,3,1,0:T(8,128)} %get-tuple-element.146, pred[]{:T(512)S(6)} %compare.5, bf16[16,257,384]{2,1,0:T(8,128)(2,1)S(1)} %reshape.63, bf16[2,64,1024]{2,1,0:T(8,128)(2,1)S(1)} %get-tuple-element.157, s32[]{:T(128)S(6)} %select_n.48), kind=kOutput, calls=%fused_computation.1.clone.1 | convolution fusion | flops 135794688 | bytes 5324805 | tf_op jit(solution)/shard_map/while/body/eval_jaxpr/ilt,mjt->milj/dot_general | solution.py:117
  145.6 6.5 %reshape.62 = bf16[16,98945]{1,0:T(8,128)(2,1)S(1)} reshape(bf16[16,257,385]{2,1,0:T(8,128)(2,1)} %broadcast_in_dim.60) | data formatting | bytes 6332480 | tf_op jit(solution)/shard_map/while/body/eval_jaxpr/reshape | solution.py:38
  156.9 4.2 %bitcast_add_fusion.2 = f32[2,16,257,64]{2,3,1,0:T(8,128)} fusion(f32[2,16,257,64]{2,3,1,0:T(8,128)} %get-tuple-element.146, pred[]{:T(512)S(6)} %compare.5, bf16[16,257,384]{2,1,0:T(8,128)(2,1)S(1)} %reshape.63, bf16[2,64,1024]{2,1,0:T(8,128)(2,1)S(1)} %get-tuple-element.157, s32[]{:T(128)S(6)} %select_n.48), kind=kOutput, calls=%fused_computation.1.clone.1 | convolution fusion | flops 135794688 | bytes 5324805 | tf_op jit(solution)/shard_map/while/body/eval_jaxpr/ilt,mjt->milj/dot_general | solution.py:117
  163.4 6.5 %reshape.62 = bf16[16,98945]{1,0:T(8,128)(2,1)S(1)} reshape(bf16[16,257,385]{2,1,0:T(8,128)(2,1)} %broadcast_in_dim.60) | data formatting | bytes 6332480 | tf_op jit(solution)/shard_map/while/body/eval_jaxpr/reshape | solution.py:38
  174.7 4.1 %bitcast_add_fusion.2 = f32[2,16,257,64]{2,3,1,0:T(8,128)} fusion(f32[2,16,257,64]{2,3,1,0:T(8,128)} %get-tuple-element.146, pred[]{:T(512)S(6)} %compare.5, bf16[16,257,384]{2,1,0:T(8,128)(2,1)S(1)} %reshape.63, bf16[2,64,1024]{2,1,0:T(8,128)(2,1)S(1)} %get-tuple-element.157, s32[]{:T(128)S(6)} %select_n.48), kind=kOutput, calls=%fused_computation.1.clone.1 | convolution fusion | flops 135794688 | bytes 5324805 | tf_op jit(solution)/shard_map/while/body/eval_jaxpr/ilt,mjt->milj/dot_general | solution.py:117
  178.8 3.4 %multiply_convert_fusion = bf16[2,16,257,64]{2,3,1,0:T(8,128)(2,1)} fusion(f32[2,16,257,64]{2,3,1,0:T(8,128)} %get-tuple-element.84), kind=kLoop, calls=%fused_computation.7 | loop fusion | flops 1052672 | bytes 3158016 | tf_op jit(solution)/shard_map/convert_element_type | solution.py:123
  182.3 3.0 %copy.7 = bf16[2,16,257,64]{3,2,1,0:T(8,128)(2,1)S(1)} copy(bf16[2,16,257,64]{2,3,1,0:T(8,128)(2,1)} %multiply_convert_fusion) | data formatting | bytes 2105344 | tf_op jit(solution)/shard_map/convert_element_type | solution.py:123
  (66 shorter events, 63.5 us)
Async XLA Ops:
  0.8 9.7 %collective-permute-start = (f32[64,96]{1,0:T(8,128)S(1)}, f32[64,96]{1,0:T(8,128)S(1)}, u32[]{:S(2)}, u32[]{:S(2)}) collective-permute-start(f32[64,96]{1,0:T(8,128)S(1)} %get-tuple-element.108), channel_id=1, source_target_pairs={{0,4},{4,8},{8,12},{1,5},{5,9},{9,13},{2,6},{6,10},{10,14},{3,7},{... | collective-permute-start | bytes 73736 | tf_op jit(solution)/shard_map/ppermute | solution.py:24
  5.8 5.8 %collective-permute-start.1 = (f32[64,96]{1,0:T(8,128)S(1)}, f32[64,96]{1,0:T(8,128)S(1)}, u32[]{:S(2)}, u32[]{:S(2)}) collective-permute-start(f32[64,96]{1,0:T(8,128)S(1)} %get-tuple-element.109), channel_id=1, source_target_pairs={{4,0},{8,4},{12,8},{5,1},{9,5},{13,9},{6,2},{10,6},{14,10},{7,3},{... | collective-permute-start | bytes 73736 | tf_op jit(solution)/shard_map/ppermute | solution.py:26
  8.8 1.6 copy-start.1
  8.8 2.8 %copy-start = (f32[64,256]{1,0:T(8,128)S(1)}, f32[64,256]{1,0:T(8,128)}, u32[]{:S(2)}) copy-start(f32[64,256]{1,0:T(8,128)} %param.5) | copy-start | bytes 196612
  18.8 20.0 %all-to-all-start = ((bf16[4,16,256]{2,1,0:T(8,128)(2,1)}), bf16[4,16,256]{2,1,0:T(8,128)(2,1)S(1)}, u32[]{:S(2)}, u32[]{:S(2)}) async-start(bf16[4,16,256]{2,1,0:T(8,128)(2,1)} %bitcast.1), calls=%async_computation | async-start | bytes 65536 | tf_op jit(solution)/shard_map/all_to_all | solution.py:104
where the time goes:
time: 188 us; the launch traced here: 187 us
  local copies, waits for them, and re-layouts  117 us (62%)
  matrix products  32.9 us (18%)
  blocking collectives  20 us (11%)
  starting transfers between devices  11.1 us (6%)
  other arithmetic  5.36 us (3%)
    reshape x9, local copies, waits for them, and re-layouts, falling(): repeated.reshape(leading + (row_count * span_width,))  52.5 us
    dot_general x8, matrix products, one_block(): jnp.einsum('ilt,mjt->milj', lagged, piece, preferred_element_type=jnp.flo...  31.3 us
    reshape x9, local copies, waits for them, and re-layouts, falling(): repeated.reshape(leading + (row_count, span_width - 1))[..., row_count - 1:]  24.4 us
    broadcast_in_dim x9, local copies, waits for them, and re-layouts, falling(): jnp.broadcast_to(extended[..., None, :], leading + (row_count, span_width))  18.3 us
    slice x8, local copies, waits for them, and re-layouts, falling(): repeated.reshape(leading + (row_count * span_width,))  14.8 us
    all_gather x1, blocking collectives, local(): incoming = lax.all_gather(partners, 'tm', axis=2, tiled=True)  14.4 us
    all_gather x1, blocking collectives, local(): lax.all_gather(normed, 'chan', axis=0, tiled=True)  5.62 us
    ppermute x1, starting transfers between devices, extended_2(): lax.ppermute(tail, axis, [(i, (i + 1) % count) for i in range(ends)])  4.92 us
  transfers between devices with their start and end apart: 3, of which 1 were waited for; matrix products, arithmetic and copies ran while one was open for 2% of the time, Pallas kernels for 0%

commit v1 on v0

v1 whole, which is shorter than its diff:
```python
import functools
import math

import jax
import jax.numpy as jnp
from jax import lax
from jax.experimental import pallas as pl
from jax.experimental.pallas import tpu as pltpu
from jax.sharding import PartitionSpec as P

AVG = 65
MAXLAG = 128
LAGS = 257
EPSILON = 1e-05

LANES = 128
ROWS = 16
BLOCK = 256
WINDOW = BLOCK + 2 * LANES
VMEM_BYTES = 56 * 1024 * 1024


def split(values):
    high = values.astype(jnp.bfloat16)
    return high, (values - high.astype(jnp.float32)).astype(jnp.bfloat16)


def mm(left, right):
    return jnp.dot(left, right, preferred_element_type=jnp.float32)


def tap_kernel(taps_ref, high_ref, low_ref, row):
    taps = taps_ref.shape[1]
    row[...] = jnp.zeros_like(row)
    row[0:1, 0:taps] = taps_ref[...]
    spread = jnp.broadcast_to(row[0:1, :], (WINDOW, WINDOW))
    shift = (taps // 2 - LANES - taps + 1) % WINDOW
    banded = pltpu.roll(spread, shift, 1, stride=1, stride_axis=0)[:, :BLOCK]
    high, low = split(banded)
    high_ref[...] = high
    low_ref[...] = low


def filter_matrix(fir_taps):
    shape = jax.ShapeDtypeStruct((WINDOW, BLOCK), jnp.bfloat16)
    return pl.pallas_call(
        tap_kernel,
        out_shape=(shape, shape),
        scratch_shapes=[pltpu.VMEM((8, WINDOW), jnp.float32)],
        name="taps",
    )(fir_taps.reshape(1, -1))


def normalize_kernel(count, at_ref, *refs):
    blocks, (high_ref, low_ref, out_ref, padded) = refs[:count], refs[count:]
    channels, samples_dev = blocks[0].shape
    samples = samples_dev * count
    edge = jnp.zeros((channels, LANES), jnp.float32)
    padded[:, :LANES] = edge
    padded[:, LANES + samples :] = edge
    for step, block in enumerate(blocks):
        start = pl.multiple_of(LANES + at_ref[step] * samples_dev, LANES)
        padded[:, pl.ds(start, samples_dev)] = block[...]
    parts = samples // BLOCK

    def windows():
        return jnp.concatenate(
            [padded[:, n * BLOCK : n * BLOCK + WINDOW] for n in range(parts)], axis=0
        )

    high, low = split(windows())
    filtered = mm(high, high_ref[...]) + (mm(high, low_ref[...]) + mm(low, high_ref[...]))
    for n in range(parts):
        padded[:, LANES + n * BLOCK : LANES + (n + 1) * BLOCK] = jnp.abs(
            filtered[n * channels : (n + 1) * channels]
        )
    high, low = split(windows())
    rows_at = lax.broadcasted_iota(jnp.int32, (WINDOW, BLOCK), 0) - LANES
    cols_at = lax.broadcasted_iota(jnp.int32, (WINDOW, BLOCK), 1)
    band = (jnp.abs(rows_at - cols_at) <= AVG // 2).astype(jnp.float32).astype(jnp.bfloat16)
    local_mean = (mm(high, band) + mm(low, band)) * (1.0 / AVG)
    normed = (filtered / (local_mean + EPSILON)).astype(jnp.bfloat16)
    for n in range(parts):
        out_ref[:, n * BLOCK : (n + 1) * BLOCK] = normed[n * channels : (n + 1) * channels]


def normalize(blocks, places, matrix):
    channels, samples_dev = blocks[0].shape
    samples = samples_dev * len(blocks)
    return pl.pallas_call(
        functools.partial(normalize_kernel, len(blocks)),
        out_shape=jax.ShapeDtypeStruct((channels, samples), jnp.bfloat16),
        in_specs=[pl.BlockSpec(memory_space=pltpu.SMEM)]
        + [pl.BlockSpec(memory_space=pltpu.VMEM)] * (len(blocks) + 2),
        out_specs=pl.BlockSpec(memory_space=pltpu.VMEM),
        scratch_shapes=[pltpu.VMEM((channels, samples + 2 * LANES), jnp.float32)],
        compiler_params=pltpu.CompilerParams(vmem_limit_bytes=VMEM_BYTES),
        name="normalize",
    )(places, *blocks, *matrix)


def correlate_kernel(at_ref, matchings_ref, groups_ref, out_ref, partner, lagged):
    match_count = matchings_ref.shape[0]
    group_ch, samples = groups_ref.shape[1:]
    group, first = at_ref[0], pl.multiple_of(at_ref[1], ROWS)
    scaling = 1.0 / math.sqrt(samples)
    pair = 2 * group_ch
    edge = jnp.zeros((group_ch, LANES), jnp.float32)
    for match in range(match_count):
        ahead = jnp.concatenate(
            [edge, groups_ref[matchings_ref[match, group]].astype(jnp.float32)], axis=1
        )
        partner[match * pair : match * pair + group_ch, :] = ahead.astype(jnp.bfloat16)
        partner[match * pair + group_ch : (match + 1) * pair, :] = pltpu.roll(
            ahead, samples + LANES - 1, 1
        ).astype(jnp.bfloat16)
    own = jnp.concatenate(
        [
            groups_ref[group, pl.ds(first, ROWS), :].astype(jnp.float32),
            jnp.zeros((ROWS, LANES), jnp.float32),
        ],
        axis=1,
    )
    turns = LANES // 2
    per_chunk = 16
    lag_pairs = (LAGS + 1) // 2
    for chunk in range(turns // per_chunk):
        for step in range(per_chunk):
            turn = chunk * per_chunk + step
            lagged[turn * ROWS : (turn + 1) * ROWS, :] = pltpu.roll(own, 2 * turn, 1).astype(
                jnp.bfloat16
            )
        for wrap in range(-(-lag_pairs // turns)):
            left = lag_pairs - wrap * turns - chunk * per_chunk
            steps = min(per_chunk, left)
            if steps <= 0:
                continue
            depth = samples + LANES - wrap * LANES
            begin = chunk * per_chunk * ROWS
            product = lax.dot_general(
                lagged[begin : begin + steps * ROWS, :depth],
                partner[:, wrap * LANES :],
                (((1,), (1,)), ((), ())),
                preferred_element_type=jnp.float32,
            )
            product = (product * scaling).astype(jnp.bfloat16)
            for step in range(steps):
                column = (wrap * turns + chunk * per_chunk + step) * pair
                width = min(pair, LAGS * group_ch - column)
                for match in range(match_count):
                    out_ref[match, :, column : column + width] = product[
                        step * ROWS : (step + 1) * ROWS, match * pair : match * pair + width
                    ]


def correlate(groups, matchings, group, first):
    match_count = matchings.shape[0]
    _, group_ch, samples = groups.shape
    vmem = pl.BlockSpec(memory_space=pltpu.VMEM)
    smem = pl.BlockSpec(memory_space=pltpu.SMEM)
    return pl.pallas_call(
        correlate_kernel,
        out_shape=jax.ShapeDtypeStruct((match_count, ROWS, LAGS * group_ch), jnp.bfloat16),
        in_specs=[smem, smem, vmem],
        out_specs=vmem,
        scratch_shapes=[
            pltpu.VMEM((2 * match_count * group_ch, samples + LANES), jnp.bfloat16),
            pltpu.VMEM((LANES // 2 * ROWS, samples + LANES), jnp.bfloat16),
        ],
        compiler_params=pltpu.CompilerParams(vmem_limit_bytes=VMEM_BYTES),
        name="correlate",
    )(jnp.stack([group, first]), matchings, groups)


def local(records, fir_taps, matchings):
    group_ch, samples_dev = records.shape
    time_count = lax.axis_size("tm")
    time_index = lax.axis_index("tm")
    group_index = lax.axis_index("chan")
    matrix = filter_matrix(fir_taps)
    blocks = [records] + [
        lax.ppermute(records, "tm", [(i, (i + s) % time_count) for i in range(time_count)])
        for s in range(1, time_count)
    ]
    places = (time_index - jnp.arange(time_count, dtype=jnp.int32)) % time_count
    normed = normalize(blocks, places, matrix)
    groups = lax.all_gather(normed, "chan", axis=0)
    row_share = group_ch // time_count
    begin = time_index * row_share
    first = begin // ROWS * ROWS
    result = correlate(groups, matchings, group_index, first)
    if row_share != ROWS:
        result = lax.dynamic_slice_in_dim(result, begin - first, row_share, 1)
    return result[:, None]


def solution(mesh):
    in_specs = (P(("parts", "chan"), "tm"), P(), P())
    out_specs = P(None, ("parts", "chan"), "tm", None)
    return jax.shard_map(local, mesh=mesh, in_specs=in_specs, out_specs=out_specs, check_vma=False)
```

time: 188 us -> 26.1 us (0.14)
  local copies, waits for them, and re-layouts: 117 us -> 0.63 us
  matrix products: 32.9 us -> 0 us
  blocking collectives: 20 us -> 8.16 us
  Pallas kernels: 0 us -> 7.94 us
  other arithmetic: 5.36 us -> 1.1 us
  starting transfers between devices: 11.1 us -> 7.86 us
    reshape x19 -> x0, local copies, waits for them, and re-layouts: 78.9 us -> none  [the longest x9 52.5 us: falling(): repeated.reshape(leading + (row_count * span_width,))]
    dot_general x10 -> x0, matrix products: 32.9 us -> none  [the longest x8 31.3 us: one_block(): jnp.einsum('ilt,mjt->milj', lagged, piece, preferred_element_type=jnp.flo...]
    broadcast_in_dim x9 -> x0, local copies, waits for them, and re-layouts: 18.3 us -> none  [falling(): jnp.broadcast_to(extended[..., None, :], leading + (row_count, span_width))]
    slice x9 -> x0, local copies, waits for them, and re-layouts: 15.7 us -> none  [the longest x8 14.8 us: falling(): repeated.reshape(leading + (row_count * span_width,))]
    all_gather x2 -> x1, blocking collectives: 20 us -> 8.16 us  [local(): groups = lax.all_gather(normed, 'chan', axis=0)]
    pallas_call x0 -> x3, Pallas kernels: none -> 7.94 us  [the longest x1 3.66 us: correlate(): pl.pallas_call(correlate_kernel, out_shape=jax.ShapeDtypeStruct((match_co...]
    all_to_all x1 -> x0, starting transfers between devices: 4.91 us -> none  [local(): lax.all_to_all(normed, 'tm', split_axis=0, concat_axis=1, tiled=True)]
    convert_element_type x1 -> x0, other arithmetic: 3.45 us -> none  [local(): (summed * scaling).astype(jnp.bfloat16)]
  transfers between devices with their start and end apart: 3 -> 3, of which waited for: 1 -> 1; matrix products, arithmetic and copies ran while one was open for 2% -> 4% of each run, Pallas kernels for 0% -> 6%
where the time goes in v1:
time: 26.1 us; the launch traced here: 25.9 us
  blocking collectives  8.16 us (31%)
  Pallas kernels  7.94 us (30%)
  starting transfers between devices  7.86 us (30%)
  other arithmetic  1.1 us (4%)
  local copies, waits for them, and re-layouts  0.63 us (2%)
    all_gather x1, blocking collectives, local(): groups = lax.all_gather(normed, 'chan', axis=0)  8.16 us
    ppermute x3, starting transfers between devices, local(): lax.ppermute(records, 'tm', [(i, (i + s) % time_count) for i in range(tim...  7.86 us
    pallas_call x1, Pallas kernels, correlate(): pl.pallas_call(correlate_kernel, out_shape=jax.ShapeDtypeStruct((match_co...  3.66 us
    pallas_call x1, Pallas kernels, normalize(): pl.pallas_call(functools.partial(normalize_kernel, len(blocks)), out_shap...  2.65 us
    pallas_call x1, Pallas kernels, filter_matrix(): pl.pallas_call(tap_kernel, out_shape=(shape, shape), scratch_shapes=[pltp...  1.62 us
    unnamed x6, local copies, waits for them, and re-layouts  0.63 us
    another operation x1, other arithmetic, correlate(): jnp.stack([group, first])  0.55 us
    select_n x1, other arithmetic, local(): places = (time_index - jnp.arange(time_count, dtype=jnp.int32)) % time_count  0.55 us
  transfers between devices with their start and end apart: 3, of which 1 were waited for; matrix products, arithmetic and copies ran while one was open for 4% of the time, Pallas kernels for 6%

profile of v1, /device:TPU:0, one launch (start us, length us, event | category | flops | bytes accessed | tf_op | source)
XLA Modules:
  0.0 25.9 jit_solution(1996387520457183427)
XLA Ops:
  0.0 4.0 %collective-permute-start.1 = (f32[64,256]{1,0:T(8,128)}, f32[64,256]{1,0:T(8,128)S(1)}, u32[]{:S(2)}, u32[]{:S(2)}) collective-permute-start(f32[64,256]{1,0:T(8,128)} %refs_0_.1), channel_id=1, source_target_pairs={{0,8},{4,12},{8,0},{12,4},{1,9},{5,13},{9,1},{13,5},{2,10},{6,14},... | collective-permute-start | bytes 196616 | tf_op jit(solution)/shard_map/ppermute | solution.py:182
  4.0 1.6 %collective-permute-start = (f32[64,256]{1,0:T(8,128)}, f32[64,256]{1,0:T(8,128)S(1)}, u32[]{:S(2)}, u32[]{:S(2)}) collective-permute-start(f32[64,256]{1,0:T(8,128)} %refs_0_.1), channel_id=1, source_target_pairs={{0,4},{4,8},{8,12},{12,0},{1,5},{5,9},{9,13},{13,1},{2,6},{6,10},{... | collective-permute-start | bytes 196616 | tf_op jit(solution)/shard_map/ppermute | solution.py:182
  5.6 2.2 %collective-permute-start.2 = (f32[64,256]{1,0:T(8,128)}, f32[64,256]{1,0:T(8,128)S(1)}, u32[]{:S(2)}, u32[]{:S(2)}) collective-permute-start(f32[64,256]{1,0:T(8,128)} %refs_0_.1), channel_id=1, source_target_pairs={{0,12},{4,0},{8,4},{12,8},{1,13},{5,1},{9,5},{13,9},{2,14},{6,2},{... | collective-permute-start | bytes 196616 | tf_op jit(solution)/shard_map/ppermute | solution.py:182
  7.9 0.6 %and_select_fusion.at_ref = s32[4]{0:T(128)} fusion(s32[]{:T(128)S(6)} %axis_index.25), kind=kLoop, calls=%fused_computation.2 | loop fusion | flops 48 | bytes 20 | tf_op jit(solution)/shard_map/jit(remainder)/select_n | solution.py:185
  8.4 1.6 %taps.1 = (bf16[512,256]{1,0:T(8,128)(2,1)}, bf16[512,256]{1,0:T(8,128)(2,1)}) custom-call(f32[1,129]{1,0:T(1,128)} %bitcast.8), custom_call_target="tpu_custom_call" | custom-call | tf_op jit(solution)/shard_map/taps/pallas_call | solution.py:46
  10.0 0.6 %pad_add_fusion.at_ref = s32[2]{0:T(128)} fusion(s32[1]{0:T(128)} %bitcast.1, s32[1]{0:T(128)} %bitcast), kind=kLoop, calls=%fused_computation.4 | loop fusion | flops 2 | bytes 16 | tf_op jit(solution)/shard_map/stack | solution.py:172
  10.6 0.0 collective-permute-done.1.refs_2_
  10.6 0.0 copy-start
  10.6 0.0 collective-permute-done.refs_1_
  10.6 0.0 copy-start.1
  10.6 0.2 collective-permute-done.2.refs_3_
  10.8 0.0 copy-start.2
  10.8 0.4 %copy-done = f32[64,256]{1,0:T(8,128)} copy-done((f32[64,256]{1,0:T(8,128)}, f32[64,256]{1,0:T(8,128)S(1)}, u32[]{:S(2)}) %copy-start) | copy-done | bytes 65560
  11.2 0.0 copy-done.1
  11.2 0.2 copy-done.2
  11.4 2.7 %normalize.1 = bf16[64,1024]{1,0:T(8,128)(2,1)} custom-call(s32[4]{0:T(128)} %and_select_fusion.at_ref, f32[64,256]{1,0:T(8,128)} %refs_0_.1, f32[64,256]{1,0:T(8,128)} %copy-done.1, f32[64,256]{1,0:T(8,128)} %copy-done, f32[64,256]{1,0:T(8,128)} %copy-done.2, bf16[512,256]{1,0:T(8,128)(2,1)} %get-tuple-element.7.refs_4_, ...), custom_call_target="tpu_custom_call" | custom-call | tf_op jit(solution)/shard_map/normalize/pallas_call | solution.py:90
  14.1 8.2 %all-gather = bf16[256,1024]{1,0:T(8,128)(2,1)} all-gather(bf16[64,1024]{1,0:T(8,128)(2,1)} %normalize.1), channel_id=2, replica_groups=mesh['parts'=2,'tm'=4,'chan'=4] {'chan'}, dimensions={0}, use_global_device_ids=true | all-gather | bytes 655360 | tf_op jit(solution)/shard_map/all_gather | solution.py:187
  22.2 3.7 %correlate.1 = bf16[2,16,16448]{2,1,0:T(8,128)(2,1)} custom-call(s32[2]{0:T(128)} %pad_add_fusion.at_ref, s32[2,4]{1,0:T(2,128)} %matchings_ref.1, bf16[4,64,1024]{2,1,0:T(8,128)(2,1)} %bitcast.7), custom_call_target="tpu_custom_call" | custom-call | tf_op jit(solution)/shard_map/correlate/pallas_call | solution.py:161
Async XLA Ops:
  0.0 10.6 %collective-permute-start.1 = (f32[64,256]{1,0:T(8,128)}, f32[64,256]{1,0:T(8,128)S(1)}, u32[]{:S(2)}, u32[]{:S(2)}) collective-permute-start(f32[64,256]{1,0:T(8,128)} %refs_0_.1), channel_id=1, source_target_pairs={{0,8},{4,12},{8,0},{12,4},{1,9},{5,13},{9,1},{13,5},{2,10},{6,14},... | collective-permute-start | bytes 196616 | tf_op jit(solution)/shard_map/ppermute | solution.py:182
  4.0 6.6 %collective-permute-start = (f32[64,256]{1,0:T(8,128)}, f32[64,256]{1,0:T(8,128)S(1)}, u32[]{:S(2)}, u32[]{:S(2)}) collective-permute-start(f32[64,256]{1,0:T(8,128)} %refs_0_.1), channel_id=1, source_target_pairs={{0,4},{4,8},{8,12},{12,0},{1,5},{5,9},{9,13},{13,1},{2,6},{6,10},{... | collective-permute-start | bytes 196616 | tf_op jit(solution)/shard_map/ppermute | solution.py:182
  5.6 5.2 %collective-permute-start.2 = (f32[64,256]{1,0:T(8,128)}, f32[64,256]{1,0:T(8,128)S(1)}, u32[]{:S(2)}, u32[]{:S(2)}) collective-permute-start(f32[64,256]{1,0:T(8,128)} %refs_0_.1), channel_id=1, source_target_pairs={{0,12},{4,0},{8,4},{12,8},{1,13},{5,1},{9,5},{13,9},{2,14},{6,2},{... | collective-permute-start | bytes 196616 | tf_op jit(solution)/shard_map/ppermute | solution.py:182
  10.6 0.6 %copy-start = (f32[64,256]{1,0:T(8,128)}, f32[64,256]{1,0:T(8,128)S(1)}, u32[]{:S(2)}) copy-start(f32[64,256]{1,0:T(8,128)S(1)} %collective-permute-done.1.refs_2_) | copy-start | bytes 196612
  10.6 0.6 %copy-start.1 = (f32[64,256]{1,0:T(8,128)}, f32[64,256]{1,0:T(8,128)S(1)}, u32[]{:S(2)}) copy-start(f32[64,256]{1,0:T(8,128)S(1)} %collective-permute-done.refs_1_) | copy-start | bytes 196612
  10.8 0.6 %copy-start.2 = (f32[64,256]{1,0:T(8,128)}, f32[64,256]{1,0:T(8,128)S(1)}, u32[]{:S(2)}) copy-start(f32[64,256]{1,0:T(8,128)S(1)} %collective-permute-done.2.refs_3_) | copy-start | bytes 196612

commit v2 on v1

v2 whole, which is shorter than its diff:
```python
import functools
import math

import jax
import jax.numpy as jnp
from jax import lax
from jax.experimental import pallas as pl
from jax.experimental.pallas import tpu as pltpu
from jax.sharding import PartitionSpec as P

AVG = 65
MAXLAG = 128
LAGS = 257
EPSILON = 1e-05

LANES = 128
ROWS = 16
BLOCK = 256
WINDOW = BLOCK + 2 * LANES
TURNS = LANES // 2
MIB = 1024 * 1024

VMEM = pl.BlockSpec(memory_space=pltpu.VMEM)
SMEM = pl.BlockSpec(memory_space=pltpu.SMEM)


def granted(*arrays):
    held = sum(math.prod(shape) * jnp.dtype(dtype).itemsize for shape, dtype in arrays)
    return pltpu.CompilerParams(vmem_limit_bytes=2 * held + 4 * MIB)


def split(values):
    high = values.astype(jnp.bfloat16)
    return high, (values - high.astype(jnp.float32)).astype(jnp.bfloat16)


def mm(left, right):
    return jnp.dot(left, right, preferred_element_type=jnp.float32)


def matrix_kernel(taps_ref, high_ref, low_ref, band_ref, row):
    taps = taps_ref.shape[1]
    row[...] = jnp.zeros_like(row)
    row[0:1, 0:taps] = taps_ref[...]
    spread = jnp.broadcast_to(row[0:1, :], (WINDOW, WINDOW))
    shift = (taps // 2 - LANES - taps + 1) % WINDOW
    banded = pltpu.roll(spread, shift, 1, stride=1, stride_axis=0)[:, :BLOCK]
    high, low = split(banded)
    high_ref[...] = high
    low_ref[...] = low
    rows_at = lax.broadcasted_iota(jnp.int32, (WINDOW, BLOCK), 0) - LANES
    cols_at = lax.broadcasted_iota(jnp.int32, (WINDOW, BLOCK), 1)
    near = jnp.abs(rows_at - cols_at) <= AVG // 2
    band_ref[...] = near.astype(jnp.float32).astype(jnp.bfloat16)


def matrices(fir_taps):
    shape = jax.ShapeDtypeStruct((WINDOW, BLOCK), jnp.bfloat16)
    return pl.pallas_call(
        matrix_kernel,
        out_shape=(shape,) * 3,
        in_specs=[VMEM],
        out_specs=(VMEM,) * 3,
        scratch_shapes=[pltpu.VMEM((8, WINDOW), jnp.float32)],
        compiler_params=granted(((WINDOW, 4 * WINDOW), jnp.float32)),
        cost_estimate=pl.CostEstimate(flops=2 * MIB, bytes_accessed=MIB, transcendentals=0),
        name="matrices",
    )(fir_taps.reshape(1, -1))


def normalize_kernel(count, *refs):
    blocks, (high_ref, low_ref, band_ref, out_ref, high, low) = refs[:count], refs[count:]
    channels, samples_dev = blocks[0].shape
    samples = samples_dev * count
    own = lax.axis_index("tm")
    edge = jnp.zeros((channels, LANES), jnp.bfloat16)
    for part in (high, low):
        part[:, :LANES] = edge
        part[:, LANES + samples :] = edge
    for step, block in enumerate(blocks):
        place = lax.rem(own + (count - step), count)
        at = pl.ds(pl.multiple_of(LANES + place * samples_dev, LANES), samples_dev)
        high[:, at], low[:, at] = split(block[...])
    parts = samples // BLOCK

    def windows(part):
        return jnp.concatenate(
            [part[:, n * BLOCK : n * BLOCK + WINDOW] for n in range(parts)], axis=0
        )

    highs, lows = windows(high), windows(low)
    filtered = mm(highs, high_ref[...]) + (mm(highs, low_ref[...]) + mm(lows, high_ref[...]))
    for n in range(parts):
        at = slice(LANES + n * BLOCK, LANES + (n + 1) * BLOCK)
        high[:, at], low[:, at] = split(jnp.abs(filtered[n * channels : (n + 1) * channels]))
    local_mean = (mm(windows(high), band_ref[...]) + mm(windows(low), band_ref[...])) * (1.0 / AVG)
    normed = (filtered / (local_mean + EPSILON)).astype(jnp.bfloat16)
    for n in range(parts):
        out_ref[:, n * BLOCK : (n + 1) * BLOCK] = normed[n * channels : (n + 1) * channels]


def normalize(blocks, banded):
    channels, samples_dev = blocks[0].shape
    samples = samples_dev * len(blocks)
    padded = (channels, samples + 2 * LANES)
    return pl.pallas_call(
        functools.partial(normalize_kernel, len(blocks)),
        out_shape=jax.ShapeDtypeStruct((channels, samples), jnp.bfloat16),
        in_specs=[VMEM] * (len(blocks) + 3),
        out_specs=VMEM,
        scratch_shapes=[pltpu.VMEM(padded, jnp.bfloat16)] * 2,
        compiler_params=granted((padded, jnp.float32), (padded, jnp.float32)),
        name="normalize",
    )(*blocks, *banded)


def lag_kernel(row_share, normed_ref, out_ref):
    first = lax.axis_index("tm") * row_share // ROWS * ROWS
    own = normed_ref[pl.ds(pl.multiple_of(first, ROWS), ROWS), :].astype(jnp.float32)
    own = jnp.concatenate([own, jnp.zeros((ROWS, LANES), jnp.float32)], axis=1)
    for turn in range(TURNS):
        out_ref[turn * ROWS : (turn + 1) * ROWS, :] = pltpu.roll(own, 2 * turn, 1).astype(
            jnp.bfloat16
        )


def lags_of(normed, row_share):
    shape = (TURNS * ROWS, normed.shape[1] + LANES)
    return pl.pallas_call(
        functools.partial(lag_kernel, row_share),
        out_shape=jax.ShapeDtypeStruct(shape, jnp.bfloat16),
        in_specs=[VMEM],
        out_specs=VMEM,
        compiler_params=granted((shape, jnp.bfloat16)),
        cost_estimate=pl.CostEstimate(flops=2 * MIB, bytes_accessed=4 * MIB, transcendentals=0),
        name="lags",
    )(normed)


def correlate_kernel(parcels, matchings_ref, lagged, *refs):
    groups, (out_ref, partner, result, sem) = refs[:parcels], refs[parcels:]
    match_count = matchings_ref.shape[0]
    group_ch, samples = groups[0].shape[-2:]
    group = lax.axis_index("chan")
    scaling = 1.0 / math.sqrt(samples)
    pair = 2 * group_ch
    edge = jnp.zeros((group_ch, LANES), jnp.float32)

    def take(match, rows):
        ahead = jnp.concatenate([edge, rows.astype(jnp.float32)], axis=1)
        partner[match * pair : match * pair + group_ch, :] = ahead.astype(jnp.bfloat16)
        partner[match * pair + group_ch : (match + 1) * pair, :] = pltpu.roll(
            ahead, samples + LANES - 1, 1
        ).astype(jnp.bfloat16)

    for match in range(match_count):
        wanted = matchings_ref[match, group]
        if parcels == 1:
            take(match, groups[0][wanted])
        else:
            for offset, held in enumerate(groups):
                pl.when((wanted ^ group) == offset)(
                    functools.partial(lambda m, h: take(m, h[...]), match, held)
                )
    lag_pairs = (LAGS + 1) // 2
    per_chunk = 16
    copies = []
    for wrap in range(-(-lag_pairs // TURNS)):
        for chunk in range(TURNS // per_chunk):
            steps = min(per_chunk, lag_pairs - wrap * TURNS - chunk * per_chunk)
            if steps <= 0:
                continue
            begin = chunk * per_chunk * ROWS
            product = lax.dot_general(
                lagged[begin : begin + steps * ROWS, : samples + LANES - wrap * LANES],
                partner[:, wrap * LANES :],
                (((1,), (1,)), ((), ())),
                preferred_element_type=jnp.float32,
            )
            product = (product * scaling).astype(jnp.bfloat16)
            left = (wrap * TURNS + chunk * per_chunk) * pair
            for step in range(steps):
                column = left + step * pair
                width = min(pair, LAGS * group_ch - column)
                for match in range(match_count):
                    result[match, :, column : column + width] = product[
                        step * ROWS : (step + 1) * ROWS, match * pair : match * pair + width
                    ]
            columns = pl.ds(left, min(steps * pair, LAGS * group_ch - left))
            copy = pltpu.make_async_copy(
                result.at[:, :, columns], out_ref.at[:, :, columns], sem.at[len(copies)]
            )
            copy.start()
            copies.append(copy)
    for copy in copies:
        copy.wait()


def correlate(matchings, lagged, groups):
    match_count = matchings.shape[0]
    group_ch, samples = groups[0].shape[-2:]
    out = (match_count, ROWS, LAGS * group_ch)
    partner = (2 * match_count * group_ch, samples + LANES)
    held = [(g.shape, g.dtype) for g in groups]
    return pl.pallas_call(
        functools.partial(correlate_kernel, len(groups)),
        out_shape=jax.ShapeDtypeStruct(out, jnp.bfloat16),
        in_specs=[SMEM, VMEM] + [VMEM] * len(groups),
        out_specs=pl.BlockSpec(memory_space=pl.ANY),
        scratch_shapes=[
            pltpu.VMEM(partner, jnp.bfloat16),
            pltpu.VMEM(out, jnp.bfloat16),
            pltpu.SemaphoreType.DMA((2 * (TURNS // ROWS) + 1,)),
        ],
        compiler_params=granted((lagged.shape, lagged.dtype), (out, jnp.bfloat16), *held),
        name="correlate",
    )(matchings, lagged, *groups)


def local(records, fir_taps, matchings):
    group_ch, samples_dev = records.shape
    time_count = lax.axis_size("tm")
    group_count = lax.axis_size("chan")
    row_share = group_ch // time_count

    def turned(cells, axis, count, step):
        return lax.ppermute(cells, axis, [(i, (i + step) % count) for i in range(count)])

    def swapped(cells, bit):
        return lax.ppermute(cells, "chan", [(i, i ^ bit) for i in range(group_count)])

    blocks = [records] + [turned(records, "tm", time_count, s) for s in range(1, time_count)]
    normed = normalize(blocks, matrices(fir_taps))
    if group_count == 4:
        far, near = swapped(normed, 2), swapped(normed, 1)
        groups = [normed, near, far, swapped(far, 1)]
    else:
        groups = [lax.all_gather(normed, "chan", axis=0)]
    result = correlate(matchings, lags_of(normed, row_share), groups)
    if row_share != ROWS:
        begin = lax.axis_index("tm") * row_share
        result = lax.dynamic_slice_in_dim(result, begin % ROWS, row_share, 1)
    return result[:, None]


def solution(mesh):
    in_specs = (P(("parts", "chan"), "tm"), P(), P())
    out_specs = P(None, ("parts", "chan"), "tm", None)
    return jax.shard_map(local, mesh=mesh, in_specs=in_specs, out_specs=out_specs, check_vma=False)
```

time: 26.1 us -> 22.1 us (0.85)
  blocking collectives: 8.16 us -> 0 us
  waiting for transfers between devices: 0.19 us -> 6.19 us
  Pallas kernels: 7.94 us -> 4.8 us
  starting transfers between devices: 7.86 us -> 9.42 us
  other arithmetic: 1.1 us -> 0 us
  local copies, waits for them, and re-layouts: 0.63 us -> 1.52 us
    all_gather x1 -> x0, blocking collectives: 8.16 us -> none  [local(): groups = lax.all_gather(normed, 'chan', axis=0)]
    ppermute x3 -> x6, waiting for transfers between devices: 0.19 us -> 6.19 us  [the longest x3 4.12 us: swapped(): lax.ppermute(cells, 'chan', [(i, i ^ bit) for i in range(group_count)])]
    pallas_call x1, Pallas kernels: 2.65 us -> 0.86 us  [normalize(): pl.pallas_call(functools.partial(normalize_kernel, len(blocks)), out_shap...]
    ppermute x3 -> x6, starting transfers between devices: 7.86 us -> 9.42 us  [the longest x3 7.86 us: turned(): lax.ppermute(cells, axis, [(i, (i + step) % count) for i in range(count)])]
    pallas_call x2 -> x3, Pallas kernels: 5.29 us -> 3.94 us  [the longest x1 3.09 us: correlate(): pl.pallas_call(functools.partial(correlate_kernel, len(groups)), out_shap...]
    unnamed x6, local copies, waits for them, and re-layouts: 0.63 us -> 1.52 us
    another operation x1 -> x0, other arithmetic: 0.55 us -> none  [correlate(): jnp.stack([group, first])]
    select_n x1 -> x0, other arithmetic: 0.55 us -> none  [local(): places = (time_index - jnp.arange(time_count, dtype=jnp.int32)) % time_count]
  transfers between devices with their start and end apart: 3 -> 6, of which waited for: 1 -> 4; matrix products, arithmetic and copies ran while one was open for 4% -> 0% of each run, Pallas kernels for 6% -> 4%
where the time goes in v2:
time: 22.1 us; the launch traced here: 22 us
  starting transfers between devices  9.42 us (43%)
  waiting for transfers between devices  6.19 us (28%)
  Pallas kernels  4.8 us (22%)
  local copies, waits for them, and re-layouts  1.52 us (7%)
    ppermute x3, starting transfers between devices, turned(): lax.ppermute(cells, axis, [(i, (i + step) % count) for i in range(count)])  7.86 us
    ppermute x3, waiting for transfers between devices, swapped(): lax.ppermute(cells, 'chan', [(i, i ^ bit) for i in range(group_count)])  4.12 us
    pallas_call x1, Pallas kernels, correlate(): pl.pallas_call(functools.partial(correlate_kernel, len(groups)), out_shap...  3.09 us
    ppermute x3, waiting for transfers between devices, turned(): lax.ppermute(cells, axis, [(i, (i + step) % count) for i in range(count)])  2.07 us
    ppermute x3, starting transfers between devices, swapped(): lax.ppermute(cells, 'chan', [(i, i ^ bit) for i in range(group_count)])  1.56 us
    unnamed x6, local copies, waits for them, and re-layouts  1.52 us
    pallas_call x1, Pallas kernels, normalize(): pl.pallas_call(functools.partial(normalize_kernel, len(blocks)), out_shap...  0.86 us
    pallas_call x1, Pallas kernels, lags_of(): pl.pallas_call(functools.partial(lag_kernel, row_share), out_shape=jax.Sh...  0.68 us
  transfers between devices with their start and end apart: 6, of which 4 were waited for; matrix products, arithmetic and copies ran while one was open for 0% of the time, Pallas kernels for 4%

profile of v2, /device:TPU:0, one launch (start us, length us, event | category | flops | bytes accessed | tf_op | source)
XLA Modules:
  0.0 22.0 jit_solution(9300178948420322986)
XLA Ops:
  0.0 0.0 copy-start.1
  0.0 4.0 %collective-permute-start.1 = (f32[64,256]{1,0:T(8,128)}, f32[64,256]{1,0:T(8,128)S(1)}, u32[]{:S(2)}, u32[]{:S(2)}) collective-permute-start(f32[64,256]{1,0:T(8,128)} %refs_0_.1), channel_id=1, source_target_pairs={{0,8},{4,12},{8,0},{12,4},{1,9},{5,13},{9,1},{13,5},{2,10},{6,14},... | collective-permute-start | bytes 196616 | tf_op jit(solution)/shard_map/ppermute | solution.py:227
  4.0 1.6 %collective-permute-start = (f32[64,256]{1,0:T(8,128)}, f32[64,256]{1,0:T(8,128)S(1)}, u32[]{:S(2)}, u32[]{:S(2)}) collective-permute-start(f32[64,256]{1,0:T(8,128)} %refs_0_.1), channel_id=1, source_target_pairs={{0,4},{4,8},{8,12},{12,0},{1,5},{5,9},{9,13},{13,1},{2,6},{6,10},{... | collective-permute-start | bytes 196616 | tf_op jit(solution)/shard_map/ppermute | solution.py:227
  5.6 2.2 %collective-permute-start.2 = (f32[64,256]{1,0:T(8,128)}, f32[64,256]{1,0:T(8,128)S(1)}, u32[]{:S(2)}, u32[]{:S(2)}) collective-permute-start(f32[64,256]{1,0:T(8,128)} %refs_0_.1), channel_id=1, source_target_pairs={{0,12},{4,0},{8,4},{12,8},{1,13},{5,1},{9,5},{13,9},{2,14},{6,2},{... | collective-permute-start | bytes 196616 | tf_op jit(solution)/shard_map/ppermute | solution.py:227
  7.9 0.0 copy-start.2
  7.9 0.7 %copy-done.2 = f32[129]{0:T(256)S(1)} copy-done((f32[129]{0:T(256)S(1)}, f32[129]{0:T(256)}, u32[]{:S(2)}) %copy-start.2) | copy-done | bytes 540
  8.5 0.2 matrices.1
  8.7 0.0 collective-permute-done.1.refs_2_
  8.7 1.7 %collective-permute-done.refs_1_ = f32[64,256]{1,0:T(8,128)S(1)} collective-permute-done((f32[64,256]{1,0:T(8,128)}, f32[64,256]{1,0:T(8,128)S(1)}, u32[]{:S(2)}, u32[]{:S(2)}) %collective-permute-start) | collective-permute-done | bytes 65568 | tf_op jit(solution)/shard_map/ppermute | solution.py:227
  10.5 0.3 %collective-permute-done.2.refs_3_ = f32[64,256]{1,0:T(8,128)S(1)} collective-permute-done((f32[64,256]{1,0:T(8,128)}, f32[64,256]{1,0:T(8,128)S(1)}, u32[]{:S(2)}, u32[]{:S(2)}) %collective-permute-start.2) | collective-permute-done | bytes 65568 | tf_op jit(solution)/shard_map/ppermute | solution.py:227
  10.8 0.0 copy-start
  10.8 0.8 %copy-done = f32[64,256]{1,0:T(8,128)S(1)} copy-done((f32[64,256]{1,0:T(8,128)S(1)}, f32[64,256]{1,0:T(8,128)}, u32[]{:S(2)}) %copy-start) | copy-done | bytes 65560
  11.6 0.9 %normalize.1.normed_ref.refs_0_ = bf16[64,1024]{1,0:T(8,128)(2,1)S(1)} custom-call(f32[64,256]{1,0:T(8,128)S(1)} %copy-done, f32[64,256]{1,0:T(8,128)S(1)} %collective-permute-done.refs_1_, f32[64,256]{1,0:T(8,128)S(1)} %collective-permute-done.1.refs_2_, f32[64,256]{1,0:T(8,128)S(1)} %collective-permute-done.2.refs_3_, ...), custom_call_target="tpu_custom_call" | custom-call | tf_op jit(solution)/shard_map/normalize/pallas_call | solution.py:106
  12.5 1.6 %collective-permute-start.4 = (bf16[64,1024]{1,0:T(8,128)(2,1)S(1)}, bf16[64,1024]{1,0:T(8,128)(2,1)S(1)}, u32[]{:S(2)}, u32[]{:S(2)}) collective-permute-start(bf16[64,1024]{1,0:T(8,128)(2,1)S(1)} %normalize.1.normed_ref.refs_0_), channel_id=1, source_target_pairs={{0,2},{1,3},{2,0},{3,1},{4,6},{5,7},{6,4},{7,5},{8,10},{9,11},{10,... | collective-permute-start | bytes 393224 | tf_op jit(solution)/shard_map/ppermute | solution.py:230
  14.1 0.0 collective-permute-start.3
  14.1 3.5 %collective-permute-done.4.refs_2_ = bf16[64,1024]{1,0:T(8,128)(2,1)S(1)} collective-permute-done((bf16[64,1024]{1,0:T(8,128)(2,1)S(1)}, bf16[64,1024]{1,0:T(8,128)(2,1)S(1)}, u32[]{:S(2)}, u32[]{:S(2)}) %collective-permute-start.4) | collective-permute-done | bytes 131104 | tf_op jit(solution)/shard_map/ppermute | solution.py:230
  17.5 0.0 collective-permute-start.5
  17.5 0.7 %lags.1.lagged = bf16[1024,1152]{1,0:T(8,128)(2,1)S(1)} custom-call(bf16[64,1024]{1,0:T(8,128)(2,1)S(1)} %normalize.1.normed_ref.refs_0_), custom_call_target="tpu_custom_call" | custom-call | flops 2097152 | bytes 4194304 | tf_op jit(solution)/shard_map/lags/pallas_call | solution.py:129
  18.2 0.0 collective-permute-done.3.refs_1_
  18.2 0.6 %collective-permute-done.5.refs_3_ = bf16[64,1024]{1,0:T(8,128)(2,1)S(1)} collective-permute-done((bf16[64,1024]{1,0:T(8,128)(2,1)S(1)}, bf16[64,1024]{1,0:T(8,128)(2,1)S(1)}, u32[]{:S(2)}, u32[]{:S(2)}) %collective-permute-start.5) | collective-permute-done | bytes 131104 | tf_op jit(solution)/shard_map/ppermute | solution.py:230
  18.9 0.0 copy-done.1
  18.9 3.1 %correlate.1 = bf16[2,16,16448]{2,1,0:T(8,128)(2,1)} custom-call(s32[2,4]{1,0:T(2,128)S(1)} %copy-done.1, bf16[1024,1152]{1,0:T(8,128)(2,1)S(1)} %lags.1.lagged, bf16[64,1024]{1,0:T(8,128)(2,1)S(1)} %normalize.1.normed_ref.refs_0_, bf16[64,1024]{1,0:T(8,128)(2,1)S(1)} %collective-permute-done.3.refs_1_, bf16[64,1024]{1,0:T(8,128)(2,1)S(1)} %collective-permute-done.4.refs_2_, ...), custom_call_target="tpu_custom_call" | custom-call | tf_op jit(solution)/shard_map/correlate/pallas_call | solution.py:205
Async XLA Ops:
  0.0 18.9 %copy-start.1 = (s32[2,4]{1,0:T(2,128)S(1)}, s32[2,4]{1,0:T(2,128)}, u32[]{:S(2)}) copy-start(s32[2,4]{1,0:T(2,128)} %matchings_ref.1) | copy-start | bytes 100
  0.0 8.7 %collective-permute-start.1 = (f32[64,256]{1,0:T(8,128)}, f32[64,256]{1,0:T(8,128)S(1)}, u32[]{:S(2)}, u32[]{:S(2)}) collective-permute-start(f32[64,256]{1,0:T(8,128)} %refs_0_.1), channel_id=1, source_target_pairs={{0,8},{4,12},{8,0},{12,4},{1,9},{5,13},{9,1},{13,5},{2,10},{6,14},... | collective-permute-start | bytes 196616 | tf_op jit(solution)/shard_map/ppermute | solution.py:227
  4.0 6.4 %collective-permute-start = (f32[64,256]{1,0:T(8,128)}, f32[64,256]{1,0:T(8,128)S(1)}, u32[]{:S(2)}, u32[]{:S(2)}) collective-permute-start(f32[64,256]{1,0:T(8,128)} %refs_0_.1), channel_id=1, source_target_pairs={{0,4},{4,8},{8,12},{12,0},{1,5},{5,9},{9,13},{13,1},{2,6},{6,10},{... | collective-permute-start | bytes 196616 | tf_op jit(solution)/shard_map/ppermute | solution.py:227
  5.6 5.2 %collective-permute-start.2 = (f32[64,256]{1,0:T(8,128)}, f32[64,256]{1,0:T(8,128)S(1)}, u32[]{:S(2)}, u32[]{:S(2)}) collective-permute-start(f32[64,256]{1,0:T(8,128)} %refs_0_.1), channel_id=1, source_target_pairs={{0,12},{4,0},{8,4},{12,8},{1,13},{5,1},{9,5},{13,9},{2,14},{6,2},{... | collective-permute-start | bytes 196616 | tf_op jit(solution)/shard_map/ppermute | solution.py:227
  7.9 0.7 %copy-start.2 = (f32[129]{0:T(256)S(1)}, f32[129]{0:T(256)}, u32[]{:S(2)}) copy-start(f32[129]{0:T(256)} %param.4) | copy-start | bytes 1552
  10.8 0.8 %copy-start = (f32[64,256]{1,0:T(8,128)S(1)}, f32[64,256]{1,0:T(8,128)}, u32[]{:S(2)}) copy-start(f32[64,256]{1,0:T(8,128)} %refs_0_.1) | copy-start | bytes 196612
  12.5 5.0 %collective-permute-start.4 = (bf16[64,1024]{1,0:T(8,128)(2,1)S(1)}, bf16[64,1024]{1,0:T(8,128)(2,1)S(1)}, u32[]{:S(2)}, u32[]{:S(2)}) collective-permute-start(bf16[64,1024]{1,0:T(8,128)(2,1)S(1)} %normalize.1.normed_ref.refs_0_), channel_id=1, source_target_pairs={{0,2},{1,3},{2,0},{3,1},{4,6},{5,7},{6,4},{7,5},{8,10},{9,11},{10,... | collective-permute-start | bytes 393224 | tf_op jit(solution)/shard_map/ppermute | solution.py:230
  14.1 4.2 %collective-permute-start.3 = (bf16[64,1024]{1,0:T(8,128)(2,1)S(1)}, bf16[64,1024]{1,0:T(8,128)(2,1)S(1)}, u32[]{:S(2)}, u32[]{:S(2)}) collective-permute-start(bf16[64,1024]{1,0:T(8,128)(2,1)S(1)} %normalize.1.normed_ref.refs_0_), channel_id=1, source_target_pairs={{0,1},{1,0},{2,3},{3,2},{4,5},{5,4},{6,7},{7,6},{8,9},{9,8},{10,11... | collective-permute-start | bytes 393224 | tf_op jit(solution)/shard_map/ppermute | solution.py:230
  17.5 1.3 %collective-permute-start.5 = (bf16[64,1024]{1,0:T(8,128)(2,1)S(1)}, bf16[64,1024]{1,0:T(8,128)(2,1)S(1)}, u32[]{:S(2)}, u32[]{:S(2)}) collective-permute-start(bf16[64,1024]{1,0:T(8,128)(2,1)S(1)} %collective-permute-done.4.refs_2_), channel_id=1, source_target_pairs={{0,1},{1,0},{2,3},{3,2},{4,5},{5,4},{6,7},{7,6},{8,9},{9,8},{10,11... | collective-permute-start | bytes 393224 | tf_op jit(solution)/shard_map/ppermute | solution.py:230

commit v3 on v2

--- a/solution.py
+++ b/solution.py
@@ -38,49 +38,75 @@
     return jnp.dot(left, right, preferred_element_type=jnp.float32)
 
 
-def matrix_kernel(taps_ref, high_ref, low_ref, band_ref, row):
-    taps = taps_ref.shape[1]
+def prepare_kernel(match_count, taps, packed_ref, *refs):
+    high_ref, low_ref, band_ref, own_high_ref, own_low_ref, slots_ref, row = refs
+    channels = own_high_ref.shape[0]
     row[...] = jnp.zeros_like(row)
-    row[0:1, 0:taps] = taps_ref[...]
+    row[0:1, 0:taps] = packed_ref[channels : channels + 1, 0:taps]
     spread = jnp.broadcast_to(row[0:1, :], (WINDOW, WINDOW))
     shift = (taps // 2 - LANES - taps + 1) % WINDOW
     banded = pltpu.roll(spread, shift, 1, stride=1, stride_axis=0)[:, :BLOCK]
-    high, low = split(banded)
-    high_ref[...] = high
-    low_ref[...] = low
+    high_ref[...], low_ref[...] = split(banded)
     rows_at = lax.broadcasted_iota(jnp.int32, (WINDOW, BLOCK), 0) - LANES
     cols_at = lax.broadcasted_iota(jnp.int32, (WINDOW, BLOCK), 1)
     near = jnp.abs(rows_at - cols_at) <= AVG // 2
     band_ref[...] = near.astype(jnp.float32).astype(jnp.bfloat16)
-
-
-def matrices(fir_taps):
-    shape = jax.ShapeDtypeStruct((WINDOW, BLOCK), jnp.bfloat16)
-    return pl.pallas_call(
-        matrix_kernel,
-        out_shape=(shape,) * 3,
+    own_high_ref[...], own_low_ref[...] = split(packed_ref[:channels, :])
+    group = lax.axis_index("chan")
+    here = lax.broadcasted_iota(jnp.int32, (1, LANES), 1) == group
+    for match in range(match_count):
+        held = packed_ref[channels + 1 + match : channels + 2 + match, :LANES]
+        wanted = jnp.sum(jnp.where(here, held, 0.0), axis=1, keepdims=True).astype(jnp.int32)
+        slot = (wanted ^ group).astype(jnp.float32)
+        slots_ref[match] = jnp.broadcast_to(slot, slots_ref.shape[1:])
+
+
+def prepare(fir_taps, records, matchings):
+    channels, width = records.shape
+    match_count, taps = matchings.shape[0], fir_taps.shape[0]
+    rows = channels + -(-(1 + match_count) // 8) * 8
+
+    def placed(cells, begin):
+        return jnp.pad(cells, ((begin, rows - begin - cells.shape[0]), (0, width - cells.shape[1])))
+
+    packed = (
+        placed(records, 0)
+        + placed(fir_taps.reshape(1, -1), channels)
+        + placed(matchings.astype(jnp.float32), channels + 1)
+    )
+    banded = jax.ShapeDtypeStruct((WINDOW, BLOCK), jnp.bfloat16)
+    own = jax.ShapeDtypeStruct(records.shape, jnp.bfloat16)
+    slots = jax.ShapeDtypeStruct((match_count, channels, LANES), jnp.float32)
+    outs = (banded,) * 3 + (own,) * 2 + (slots,)
+    return pl.pallas_call(
+        functools.partial(prepare_kernel, match_count, taps),
+        out_shape=outs,
         in_specs=[VMEM],
-        out_specs=(VMEM,) * 3,
+        out_specs=(VMEM,) * len(outs),
         scratch_shapes=[pltpu.VMEM((8, WINDOW), jnp.float32)],
         compiler_params=granted(((WINDOW, 4 * WINDOW), jnp.float32)),
         cost_estimate=pl.CostEstimate(flops=2 * MIB, bytes_accessed=MIB, transcendentals=0),
-        name="matrices",
-    )(fir_taps.reshape(1, -1))
-
-
-def normalize_kernel(count, *refs):
-    blocks, (high_ref, low_ref, band_ref, out_ref, high, low) = refs[:count], refs[count:]
-    channels, samples_dev = blocks[0].shape
+        name="prepare",
+    )(packed)
+
+
+def normalize_kernel(steps, own_high, own_low, high_ref, low_ref, band_ref, *refs):
+    blocks, (out_ref, high, low) = refs[:-3], refs[-3:]
+    channels, samples_dev = own_high.shape
+    count = len(blocks) + 1
     samples = samples_dev * count
     own = lax.axis_index("tm")
     edge = jnp.zeros((channels, LANES), jnp.bfloat16)
     for part in (high, low):
         part[:, :LANES] = edge
         part[:, LANES + samples :] = edge
-    for step, block in enumerate(blocks):
+    for step, block in zip((0, *steps), (None, *blocks)):
         place = lax.rem(own + (count - step), count)
         at = pl.ds(pl.multiple_of(LANES + place * samples_dev, LANES), samples_dev)
-        high[:, at], low[:, at] = split(block[...])
+        if step == 0:
+            high[:, at], low[:, at] = own_high[...], own_low[...]
+        else:
+            high[:, at], low[:, at] = split(block[...])
     parts = samples // BLOCK
 
     def windows(part):
@@ -99,19 +125,19 @@
         out_ref[:, n * BLOCK : (n + 1) * BLOCK] = normed[n * channels : (n + 1) * channels]
 
 
-def normalize(blocks, banded):
-    channels, samples_dev = blocks[0].shape
-    samples = samples_dev * len(blocks)
+def normalize(own, banded, steps, blocks):
+    channels, samples_dev = own[0].shape
+    samples = samples_dev * (len(blocks) + 1)
     padded = (channels, samples + 2 * LANES)
     return pl.pallas_call(
-        functools.partial(normalize_kernel, len(blocks)),
+        functools.partial(normalize_kernel, steps),
         out_shape=jax.ShapeDtypeStruct((channels, samples), jnp.bfloat16),
-        in_specs=[VMEM] * (len(blocks) + 3),
+        in_specs=[VMEM] * (len(blocks) + 5),
         out_specs=VMEM,
         scratch_shapes=[pltpu.VMEM(padded, jnp.bfloat16)] * 2,
         compiler_params=granted((padded, jnp.float32), (padded, jnp.float32)),
         name="normalize",
-    )(*blocks, *banded)
+    )(*own, *banded, *blocks)
 
 
 def lag_kernel(row_share, normed_ref, out_ref):
@@ -137,11 +163,10 @@
     )(normed)
 
 
-def correlate_kernel(parcels, matchings_ref, lagged, *refs):
+def correlate_kernel(parcels, picks_ref, lagged, *refs):
     groups, (out_ref, partner, result, sem) = refs[:parcels], refs[parcels:]
-    match_count = matchings_ref.shape[0]
+    match_count = picks_ref.shape[0]
     group_ch, samples = groups[0].shape[-2:]
-    group = lax.axis_index("chan")
     scaling = 1.0 / math.sqrt(samples)
     pair = 2 * group_ch
     edge = jnp.zeros((group_ch, LANES), jnp.float32)
@@ -154,14 +179,18 @@
         ).astype(jnp.bfloat16)
 
     for match in range(match_count):
-        wanted = matchings_ref[match, group]
         if parcels == 1:
-            take(match, groups[0][wanted])
-        else:
-            for offset, held in enumerate(groups):
-                pl.when((wanted ^ group) == offset)(
-                    functools.partial(lambda m, h: take(m, h[...]), match, held)
-                )
+            take(match, groups[0][picks_ref[match, lax.axis_index("chan")]])
+            continue
+        slot = picks_ref[match]
+        tiles = []
+        for begin in range(0, samples, LANES):
+            tile = groups[-1][:, begin : begin + LANES].astype(jnp.float32)
+            for offset in range(parcels - 1):
+                held = groups[offset][:, begin : begin + LANES].astype(jnp.float32)
+                tile = jnp.where(slot == offset + 1.0, held, tile)
+            tiles.append(tile)
+        take(match, jnp.concatenate(tiles, axis=1))
     lag_pairs = (LAGS + 1) // 2
     per_chunk = 16
     copies = []
@@ -196,8 +225,8 @@
         copy.wait()
 
 
-def correlate(matchings, lagged, groups):
-    match_count = matchings.shape[0]
+def correlate(picks, lagged, groups):
+    match_count = picks.shape[0]
     group_ch, samples = groups[0].shape[-2:]
     out = (match_count, ROWS, LAGS * group_ch)
     partner = (2 * match_count * group_ch, samples + LANES)
@@ -205,7 +234,7 @@
     return pl.pallas_call(
         functools.partial(correlate_kernel, len(groups)),
         out_shape=jax.ShapeDtypeStruct(out, jnp.bfloat16),
-        in_specs=[SMEM, VMEM] + [VMEM] * len(groups),
+        in_specs=[SMEM if len(groups) == 1 else VMEM, VMEM] + [VMEM] * len(groups),
         out_specs=pl.BlockSpec(memory_space=pl.ANY),
         scratch_shapes=[
             pltpu.VMEM(partner, jnp.bfloat16),
@@ -214,7 +243,7 @@
         ],
         compiler_params=granted((lagged.shape, lagged.dtype), (out, jnp.bfloat16), *held),
         name="correlate",
-    )(matchings, lagged, *groups)
+    )(picks, lagged, *groups)
 
 
 def local(records, fir_taps, matchings):
@@ -229,14 +258,16 @@
     def swapped(cells, bit):
         return lax.ppermute(cells, "chan", [(i, i ^ bit) for i in range(group_count)])
 
-    blocks = [records] + [turned(records, "tm", time_count, s) for s in range(1, time_count)]
-    normed = normalize(blocks, matrices(fir_taps))
+    steps = sorted(range(1, time_count), key=lambda step: (min(step, time_count - step), step % 2 * step))
+    blocks = [turned(records, "tm", time_count, step) for step in steps]
+    *banded, own_high, own_low, slots = prepare(fir_taps, records, matchings)
+    normed = normalize((own_high, own_low), banded, steps, blocks)
     if group_count == 4:
-        far, near = swapped(normed, 2), swapped(normed, 1)
-        groups = [normed, near, far, swapped(far, 1)]
+        near, far = swapped(normed, 1), swapped(normed, 2)
+        picks, groups = slots, [near, far, swapped(far, 1)]
     else:
-        groups = [lax.all_gather(normed, "chan", axis=0)]
-    result = correlate(matchings, lags_of(normed, row_share), groups)
+        picks, groups = matchings, [lax.all_gather(normed, "chan", axis=0)]
+    result = correlate(picks, lags_of(normed, row_share), groups)
     if row_share != ROWS:
         begin = lax.axis_index("tm") * row_share
         result = lax.dynamic_slice_in_dim(result, begin % ROWS, row_share, 1)

time: 22.1 us -> 20.4 us (0.923)
  other arithmetic: 0 us -> 1.54 us
  local copies, waits for them, and re-layouts: 1.52 us -> 0 us
  starting transfers between devices: 9.42 us -> 8.57 us
  Pallas kernels: 4.8 us -> 4.17 us
  waiting for transfers between devices: 6.19 us -> 5.92 us
    unnamed x6 -> x0, local copies, waits for them, and re-layouts: 1.52 us -> none
    ppermute x3, starting transfers between devices: 7.86 us -> 6.96 us  [turned(): lax.ppermute(cells, axis, [(i, (i + step) % count) for i in range(count)])]
    add x0 -> x1, other arithmetic: none -> 0.86 us  [prepare(): placed(records, 0) + placed(fir_taps.reshape(1, -1), channels)]
    convert_element_type x0 -> x1, other arithmetic: none -> 0.68 us  [prepare(): matchings.astype(jnp.float32)]
    pallas_call x1, Pallas kernels: 3.09 us -> 2.44 us  [correlate(): pl.pallas_call(functools.partial(correlate_kernel, len(groups)), out_shap...]
    ppermute x3, waiting for transfers between devices: 2.07 us -> 1.82 us  [turned(): lax.ppermute(cells, axis, [(i, (i + step) % count) for i in range(count)])]
  transfers between devices with their start and end apart: 6 -> 6, of which waited for: 4 -> 4; matrix products, arithmetic and copies ran while one was open for 0% -> 8% of each run, Pallas kernels for 4% -> 4%
where the time goes in v3:
time: 20.4 us; the launch traced here: 20.2 us
  starting transfers between devices  8.57 us (42%)
  waiting for transfers between devices  5.92 us (29%)
  Pallas kernels  4.17 us (20%)
  other arithmetic  1.54 us (8%)
    ppermute x3, starting transfers between devices, turned(): lax.ppermute(cells, axis, [(i, (i + step) % count) for i in range(count)])  6.96 us
    ppermute x3, waiting for transfers between devices, swapped(): lax.ppermute(cells, 'chan', [(i, i ^ bit) for i in range(group_count)])  4.09 us
    pallas_call x1, Pallas kernels, correlate(): pl.pallas_call(functools.partial(correlate_kernel, len(groups)), out_shap...  2.44 us
    ppermute x3, waiting for transfers between devices, turned(): lax.ppermute(cells, axis, [(i, (i + step) % count) for i in range(count)])  1.82 us
    ppermute x3, starting transfers between devices, swapped(): lax.ppermute(cells, 'chan', [(i, i ^ bit) for i in range(group_count)])  1.61 us
    add x1, other arithmetic, prepare(): placed(records, 0) + placed(fir_taps.reshape(1, -1), channels)  0.86 us
    pallas_call x1, Pallas kernels, normalize(): pl.pallas_call(functools.partial(normalize_kernel, steps), out_shape=jax....  0.86 us
    pallas_call x1, Pallas kernels, lags_of(): pl.pallas_call(functools.partial(lag_kernel, row_share), out_shape=jax.Sh...  0.68 us
  transfers between devices with their start and end apart: 6, of which 4 were waited for; matrix products, arithmetic and copies ran while one was open for 8% of the time, Pallas kernels for 4%

profile of v3, /device:TPU:0, one launch (start us, length us, event | category | flops | bytes accessed | tf_op | source)
XLA Modules:
  0.0 20.2 jit_solution(17304444773163140100)
XLA Ops:
  0.0 3.0 %collective-permute-start = (f32[64,256]{1,0:T(8,128)}, f32[64,256]{1,0:T(8,128)S(1)}, u32[]{:S(2)}, u32[]{:S(2)}) collective-permute-start(f32[64,256]{1,0:T(8,128)} %param.3), channel_id=1, source_target_pairs={{0,4},{4,8},{8,12},{12,0},{1,5},{5,9},{9,13},{13,1},{2,6},{6,10},{... | collective-permute-start | bytes 196616 | tf_op jit(solution)/shard_map/ppermute | solution.py:256
  3.0 2.6 %collective-permute-start.2 = (f32[64,256]{1,0:T(8,128)}, f32[64,256]{1,0:T(8,128)S(1)}, u32[]{:S(2)}, u32[]{:S(2)}) collective-permute-start(f32[64,256]{1,0:T(8,128)} %param.3), channel_id=1, source_target_pairs={{0,8},{4,12},{8,0},{12,4},{1,9},{5,13},{9,1},{13,5},{2,10},{6,14},... | collective-permute-start | bytes 196616 | tf_op jit(solution)/shard_map/ppermute | solution.py:256
  5.6 1.3 %collective-permute-start.1 = (f32[64,256]{1,0:T(8,128)}, f32[64,256]{1,0:T(8,128)S(1)}, u32[]{:S(2)}, u32[]{:S(2)}) collective-permute-start(f32[64,256]{1,0:T(8,128)} %param.3), channel_id=1, source_target_pairs={{0,12},{4,0},{8,4},{12,8},{1,13},{5,1},{9,5},{13,9},{2,14},{6,2},{... | collective-permute-start | bytes 196616 | tf_op jit(solution)/shard_map/ppermute | solution.py:256
  7.0 0.7 %convert_element_type.9 = f32[2,4]{1,0:T(2,128)S(1)} convert(s32[2,4]{1,0:T(2,128)} %param.5) | non-fusion elementwise | flops 8 | bytes 64 | tf_op jit(solution)/shard_map/convert_element_type | solution.py:75
  7.6 0.9 %pad_add_fusion.packed_ref = f32[72,256]{1,0:T(8,128)S(1)} fusion(f32[2,4]{1,0:T(2,128)S(1)} %convert_element_type.9, f32[1,129]{1,0:T(1,128)} %bitcast.4, f32[64,256]{1,0:T(8,128)} %param.3), kind=kLoop, calls=%fused_computation | loop fusion | flops 36864 | bytes 139812 | tf_op jit(solution)/shard_map/add | solution.py:73
  8.5 0.2 prepare.1
  8.7 0.0 collective-permute-done.refs_0_
  8.7 1.6 %collective-permute-done.2.refs_2_ = f32[64,256]{1,0:T(8,128)S(1)} collective-permute-done((f32[64,256]{1,0:T(8,128)}, f32[64,256]{1,0:T(8,128)S(1)}, u32[]{:S(2)}, u32[]{:S(2)}) %collective-permute-start.2) | collective-permute-done | bytes 65568 | tf_op jit(solution)/shard_map/ppermute | solution.py:256
  10.3 0.2 %collective-permute-done.1.refs_1_ = f32[64,256]{1,0:T(8,128)S(1)} collective-permute-done((f32[64,256]{1,0:T(8,128)}, f32[64,256]{1,0:T(8,128)S(1)}, u32[]{:S(2)}, u32[]{:S(2)}) %collective-permute-start.1) | collective-permute-done | bytes 65568 | tf_op jit(solution)/shard_map/ppermute | solution.py:256
  10.5 0.9 %normalize.1.normed_ref = bf16[64,1024]{1,0:T(8,128)(2,1)S(1)} custom-call(bf16[64,256]{1,0:T(8,128)(2,1)S(1)} %get-tuple-element.12.own_high, bf16[64,256]{1,0:T(8,128)(2,1)S(1)} %get-tuple-element.13.own_low, bf16[512,256]{1,0:T(8,128)(2,1)S(1)} %get-tuple-element.14.high_ref, bf16[512,256]{1,0:T(8,128)(2,1)S(1)} %get-tuple-element.15.low_ref, ...), custom_call_target="tpu_custom_call" | custom-call | tf_op jit(solution)/shard_map/normalize/pallas_call | solution.py:132
  11.4 1.6 %collective-permute-start.4 = (bf16[64,1024]{1,0:T(8,128)(2,1)S(1)}, bf16[64,1024]{1,0:T(8,128)(2,1)S(1)}, u32[]{:S(2)}, u32[]{:S(2)}) collective-permute-start(bf16[64,1024]{1,0:T(8,128)(2,1)S(1)} %normalize.1.normed_ref), channel_id=1, source_target_pairs={{0,2},{1,3},{2,0},{3,1},{4,6},{5,7},{6,4},{7,5},{8,10},{9,11},{10,... | collective-permute-start | bytes 393224 | tf_op jit(solution)/shard_map/ppermute | solution.py:259
  13.0 0.0 collective-permute-start.3
  13.0 3.4 %collective-permute-done.4.refs_1_ = bf16[64,1024]{1,0:T(8,128)(2,1)S(1)} collective-permute-done((bf16[64,1024]{1,0:T(8,128)(2,1)S(1)}, bf16[64,1024]{1,0:T(8,128)(2,1)S(1)}, u32[]{:S(2)}, u32[]{:S(2)}) %collective-permute-start.4) | collective-permute-done | bytes 131104 | tf_op jit(solution)/shard_map/ppermute | solution.py:259
  16.5 0.0 collective-permute-start.5
  16.5 0.7 %lags.1.lagged = bf16[1024,1152]{1,0:T(8,128)(2,1)S(1)} custom-call(bf16[64,1024]{1,0:T(8,128)(2,1)S(1)} %normalize.1.normed_ref), custom_call_target="tpu_custom_call" | custom-call | flops 2097152 | bytes 4194304 | tf_op jit(solution)/shard_map/lags/pallas_call | solution.py:155
  17.1 0.0 collective-permute-done.3.refs_0_
  17.2 0.6 %collective-permute-done.5.refs_2_ = bf16[64,1024]{1,0:T(8,128)(2,1)S(1)} collective-permute-done((bf16[64,1024]{1,0:T(8,128)(2,1)S(1)}, bf16[64,1024]{1,0:T(8,128)(2,1)S(1)}, u32[]{:S(2)}, u32[]{:S(2)}) %collective-permute-start.5) | collective-permute-done | bytes 131104 | tf_op jit(solution)/shard_map/ppermute | solution.py:259
  17.8 2.4 %correlate.1 = bf16[2,16,16448]{2,1,0:T(8,128)(2,1)} custom-call(f32[2,64,128]{2,1,0:T(8,128)S(1)} %get-tuple-element.11.picks_ref, bf16[1024,1152]{1,0:T(8,128)(2,1)S(1)} %lags.1.lagged, bf16[64,1024]{1,0:T(8,128)(2,1)S(1)} %collective-permute-done.3.refs_0_, bf16[64,1024]{1,0:T(8,128)(2,1)S(1)} %collective-permute-done.4.refs_1_, ...), custom_call_target="tpu_custom_call" | custom-call | tf_op jit(solution)/shard_map/correlate/pallas_call | solution.py:234
Async XLA Ops:
  0.0 8.7 %collective-permute-start = (f32[64,256]{1,0:T(8,128)}, f32[64,256]{1,0:T(8,128)S(1)}, u32[]{:S(2)}, u32[]{:S(2)}) collective-permute-start(f32[64,256]{1,0:T(8,128)} %param.3), channel_id=1, source_target_pairs={{0,4},{4,8},{8,12},{12,0},{1,5},{5,9},{9,13},{13,1},{2,6},{6,10},{... | collective-permute-start | bytes 196616 | tf_op jit(solution)/shard_map/ppermute | solution.py:256
  3.0 7.3 %collective-permute-start.2 = (f32[64,256]{1,0:T(8,128)}, f32[64,256]{1,0:T(8,128)S(1)}, u32[]{:S(2)}, u32[]{:S(2)}) collective-permute-start(f32[64,256]{1,0:T(8,128)} %param.3), channel_id=1, source_target_pairs={{0,8},{4,12},{8,0},{12,4},{1,9},{5,13},{9,1},{13,5},{2,10},{6,14},... | collective-permute-start | bytes 196616 | tf_op jit(solution)/shard_map/ppermute | solution.py:256
  5.6 4.9 %collective-permute-start.1 = (f32[64,256]{1,0:T(8,128)}, f32[64,256]{1,0:T(8,128)S(1)}, u32[]{:S(2)}, u32[]{:S(2)}) collective-permute-start(f32[64,256]{1,0:T(8,128)} %param.3), channel_id=1, source_target_pairs={{0,12},{4,0},{8,4},{12,8},{1,13},{5,1},{9,5},{13,9},{2,14},{6,2},{... | collective-permute-start | bytes 196616 | tf_op jit(solution)/shard_map/ppermute | solution.py:256
  11.4 5.1 %collective-permute-start.4 = (bf16[64,1024]{1,0:T(8,128)(2,1)S(1)}, bf16[64,1024]{1,0:T(8,128)(2,1)S(1)}, u32[]{:S(2)}, u32[]{:S(2)}) collective-permute-start(bf16[64,1024]{1,0:T(8,128)(2,1)S(1)} %normalize.1.normed_ref), channel_id=1, source_target_pairs={{0,2},{1,3},{2,0},{3,1},{4,6},{5,7},{6,4},{7,5},{8,10},{9,11},{10,... | collective-permute-start | bytes 393224 | tf_op jit(solution)/shard_map/ppermute | solution.py:259
  13.0 4.1 %collective-permute-start.3 = (bf16[64,1024]{1,0:T(8,128)(2,1)S(1)}, bf16[64,1024]{1,0:T(8,128)(2,1)S(1)}, u32[]{:S(2)}, u32[]{:S(2)}) collective-permute-start(bf16[64,1024]{1,0:T(8,128)(2,1)S(1)} %normalize.1.normed_ref), channel_id=1, source_target_pairs={{0,1},{1,0},{2,3},{3,2},{4,5},{5,4},{6,7},{7,6},{8,9},{9,8},{10,11... | collective-permute-start | bytes 393224 | tf_op jit(solution)/shard_map/ppermute | solution.py:259
  16.5 1.3 %collective-permute-start.5 = (bf16[64,1024]{1,0:T(8,128)(2,1)S(1)}, bf16[64,1024]{1,0:T(8,128)(2,1)S(1)}, u32[]{:S(2)}, u32[]{:S(2)}) collective-permute-start(bf16[64,1024]{1,0:T(8,128)(2,1)S(1)} %collective-permute-done.4.refs_1_), channel_id=1, source_target_pairs={{0,1},{1,0},{2,3},{3,2},{4,5},{5,4},{6,7},{7,6},{8,9},{9,8},{10,11... | collective-permute-start | bytes 393224 | tf_op jit(solution)/shard_map/ppermute | solution.py:259

commit v4 on v3

--- a/solution.py
+++ b/solution.py
@@ -58,7 +58,7 @@
         held = packed_ref[channels + 1 + match : channels + 2 + match, :LANES]
         wanted = jnp.sum(jnp.where(here, held, 0.0), axis=1, keepdims=True).astype(jnp.int32)
         slot = (wanted ^ group).astype(jnp.float32)
-        slots_ref[match] = jnp.broadcast_to(slot, slots_ref.shape[1:])
+        slots_ref[match] = jnp.broadcast_to(slot, slots_ref.shape[1:]).astype(jnp.bfloat16)
 
 
 def prepare(fir_taps, records, matchings):
@@ -76,7 +76,7 @@
     )
     banded = jax.ShapeDtypeStruct((WINDOW, BLOCK), jnp.bfloat16)
     own = jax.ShapeDtypeStruct(records.shape, jnp.bfloat16)
-    slots = jax.ShapeDtypeStruct((match_count, channels, LANES), jnp.float32)
+    slots = jax.ShapeDtypeStruct((match_count, channels, LANES), jnp.bfloat16)
     outs = (banded,) * 3 + (own,) * 2 + (slots,)
     return pl.pallas_call(
         functools.partial(prepare_kernel, match_count, taps),
@@ -144,10 +144,14 @@
     first = lax.axis_index("tm") * row_share // ROWS * ROWS
     own = normed_ref[pl.ds(pl.multiple_of(first, ROWS), ROWS), :].astype(jnp.float32)
     own = jnp.concatenate([own, jnp.zeros((ROWS, LANES), jnp.float32)], axis=1)
+    last = lax.broadcasted_iota(jnp.int32, (ROWS, LANES), 1) == LANES - 1
+    samples = normed_ref.shape[1]
     for turn in range(TURNS):
-        out_ref[turn * ROWS : (turn + 1) * ROWS, :] = pltpu.roll(own, 2 * turn, 1).astype(
-            jnp.bfloat16
-        )
+        moved = pltpu.roll(own, 2 * turn, 1)
+        tail = jnp.where(last, moved[:, :LANES], moved[:, samples:])
+        at = slice(turn * ROWS, (turn + 1) * ROWS)
+        out_ref[at, :samples] = moved[:, :samples].astype(jnp.bfloat16)
+        out_ref[at, samples:] = tail.astype(jnp.bfloat16)
 
 
 def lags_of(normed, row_share):
@@ -169,14 +173,19 @@
     group_ch, samples = groups[0].shape[-2:]
     scaling = 1.0 / math.sqrt(samples)
     pair = 2 * group_ch
-    edge = jnp.zeros((group_ch, LANES), jnp.float32)
+    last = lax.broadcasted_iota(jnp.int32, (group_ch, LANES), 1) == LANES - 1
 
     def take(match, rows):
-        ahead = jnp.concatenate([edge, rows.astype(jnp.float32)], axis=1)
-        partner[match * pair : match * pair + group_ch, :] = ahead.astype(jnp.bfloat16)
-        partner[match * pair + group_ch : (match + 1) * pair, :] = pltpu.roll(
-            ahead, samples + LANES - 1, 1
-        ).astype(jnp.bfloat16)
+        even, odd = pl.ds(match * pair, group_ch), pl.ds(match * pair + group_ch, group_ch)
+        ahead = pltpu.roll(rows.astype(jnp.float32), samples - 1, 1)
+        body, end = slice(0, samples - LANES), slice(samples - LANES, samples)
+        for wrap in range(2):
+            partner[wrap, even, body] = rows[:, body].astype(jnp.bfloat16)
+            partner[wrap, odd, body] = ahead[:, body].astype(jnp.bfloat16)
+        partner[1, even, end] = rows[:, end].astype(jnp.bfloat16)
+        partner[0, odd, end] = ahead[:, end].astype(jnp.bfloat16)
+        partner[0, even, end] = jnp.where(last, 0.0, rows[:, end].astype(jnp.float32)).astype(jnp.bfloat16)
+        partner[1, odd, end] = jnp.where(last, 0.0, ahead[:, end]).astype(jnp.bfloat16)
 
     for match in range(match_count):
         if parcels == 1:
@@ -185,9 +194,9 @@
         slot = picks_ref[match]
         tiles = []
         for begin in range(0, samples, LANES):
-            tile = groups[-1][:, begin : begin + LANES].astype(jnp.float32)
+            tile = groups[-1][:, begin : begin + LANES]
             for offset in range(parcels - 1):
-                held = groups[offset][:, begin : begin + LANES].astype(jnp.float32)
+                held = groups[offset][:, begin : begin + LANES]
                 tile = jnp.where(slot == offset + 1.0, held, tile)
             tiles.append(tile)
         take(match, jnp.concatenate(tiles, axis=1))
@@ -200,9 +209,11 @@
             if steps <= 0:
                 continue
             begin = chunk * per_chunk * ROWS
+            skip = max(wrap - 1, 0) * LANES
+            first = LANES if wrap == 0 else 0
             product = lax.dot_general(
-                lagged[begin : begin + steps * ROWS, : samples + LANES - wrap * LANES],
-                partner[:, wrap * LANES :],
+                lagged[begin : begin + steps * ROWS, first : first + samples - skip],
+                partner[min(wrap, 1), :, skip:],
                 (((1,), (1,)), ((), ())),
                 preferred_element_type=jnp.float32,
             )
@@ -229,7 +240,7 @@
     match_count = picks.shape[0]
     group_ch, samples = groups[0].shape[-2:]
     out = (match_count, ROWS, LAGS * group_ch)
-    partner = (2 * match_count * group_ch, samples + LANES)
+    partner = (2, 2 * match_count * group_ch, samples)
     held = [(g.shape, g.dtype) for g in groups]
     return pl.pallas_call(
         functools.partial(correlate_kernel, len(groups)),

time: 20.4 us -> 20.3 us (level)
  no operation moved by 1% of the time
where the time goes in v4:
time: 20.3 us; the launch traced here: 20.1 us
  starting transfers between devices  8.57 us (42%)
  waiting for transfers between devices  5.92 us (29%)
  Pallas kernels  4.02 us (20%)
  other arithmetic  1.54 us (8%)
    ppermute x3, starting transfers between devices, turned(): lax.ppermute(cells, axis, [(i, (i + step) % count) for i in range(count)])  6.96 us
    ppermute x3, waiting for transfers between devices, swapped(): lax.ppermute(cells, 'chan', [(i, i ^ bit) for i in range(group_count)])  4.1 us
    pallas_call x1, Pallas kernels, correlate(): pl.pallas_call(functools.partial(correlate_kernel, len(groups)), out_shap...  2.28 us
    ppermute x3, waiting for transfers between devices, turned(): lax.ppermute(cells, axis, [(i, (i + step) % count) for i in range(count)])  1.82 us
    ppermute x3, starting transfers between devices, swapped(): lax.ppermute(cells, 'chan', [(i, i ^ bit) for i in range(group_count)])  1.61 us
    add x1, other arithmetic, prepare(): placed(records, 0) + placed(fir_taps.reshape(1, -1), channels)  0.86 us
    pallas_call x1, Pallas kernels, normalize(): pl.pallas_call(functools.partial(normalize_kernel, steps), out_shape=jax....  0.86 us
    pallas_call x1, Pallas kernels, lags_of(): pl.pallas_call(functools.partial(lag_kernel, row_share), out_shape=jax.Sh...  0.68 us
  transfers between devices with their start and end apart: 6, of which 4 were waited for; matrix products, arithmetic and copies ran while one was open for 8% of the time, Pallas kernels for 4%

profile of v4, /device:TPU:0, one launch (start us, length us, event | category | flops | bytes accessed | tf_op | source)
XLA Modules:
  0.0 20.1 jit_solution(9518986315534533348)
XLA Ops:
  0.0 3.0 %collective-permute-start = (f32[64,256]{1,0:T(8,128)}, f32[64,256]{1,0:T(8,128)S(1)}, u32[]{:S(2)}, u32[]{:S(2)}) collective-permute-start(f32[64,256]{1,0:T(8,128)} %param.3), channel_id=1, source_target_pairs={{0,4},{4,8},{8,12},{12,0},{1,5},{5,9},{9,13},{13,1},{2,6},{6,10},{... | collective-permute-start | bytes 196616 | tf_op jit(solution)/shard_map/ppermute | solution.py:267
  3.0 2.6 %collective-permute-start.2 = (f32[64,256]{1,0:T(8,128)}, f32[64,256]{1,0:T(8,128)S(1)}, u32[]{:S(2)}, u32[]{:S(2)}) collective-permute-start(f32[64,256]{1,0:T(8,128)} %param.3), channel_id=1, source_target_pairs={{0,8},{4,12},{8,0},{12,4},{1,9},{5,13},{9,1},{13,5},{2,10},{6,14},... | collective-permute-start | bytes 196616 | tf_op jit(solution)/shard_map/ppermute | solution.py:267
  5.6 1.3 %collective-permute-start.1 = (f32[64,256]{1,0:T(8,128)}, f32[64,256]{1,0:T(8,128)S(1)}, u32[]{:S(2)}, u32[]{:S(2)}) collective-permute-start(f32[64,256]{1,0:T(8,128)} %param.3), channel_id=1, source_target_pairs={{0,12},{4,0},{8,4},{12,8},{1,13},{5,1},{9,5},{13,9},{2,14},{6,2},{... | collective-permute-start | bytes 196616 | tf_op jit(solution)/shard_map/ppermute | solution.py:267
  7.0 0.7 %convert_element_type.9 = f32[2,4]{1,0:T(2,128)S(1)} convert(s32[2,4]{1,0:T(2,128)} %param.5) | non-fusion elementwise | flops 8 | bytes 64 | tf_op jit(solution)/shard_map/convert_element_type | solution.py:75
  7.6 0.9 %pad_add_fusion.packed_ref = f32[72,256]{1,0:T(8,128)S(1)} fusion(f32[2,4]{1,0:T(2,128)S(1)} %convert_element_type.9, f32[1,129]{1,0:T(1,128)} %bitcast.4, f32[64,256]{1,0:T(8,128)} %param.3), kind=kLoop, calls=%fused_computation | loop fusion | flops 36864 | bytes 139812 | tf_op jit(solution)/shard_map/add | solution.py:73
  8.5 0.2 prepare.1
  8.7 0.0 collective-permute-done.refs_0_
  8.7 1.6 %collective-permute-done.2.refs_2_ = f32[64,256]{1,0:T(8,128)S(1)} collective-permute-done((f32[64,256]{1,0:T(8,128)}, f32[64,256]{1,0:T(8,128)S(1)}, u32[]{:S(2)}, u32[]{:S(2)}) %collective-permute-start.2) | collective-permute-done | bytes 65568 | tf_op jit(solution)/shard_map/ppermute | solution.py:267
  10.3 0.2 %collective-permute-done.1.refs_1_ = f32[64,256]{1,0:T(8,128)S(1)} collective-permute-done((f32[64,256]{1,0:T(8,128)}, f32[64,256]{1,0:T(8,128)S(1)}, u32[]{:S(2)}, u32[]{:S(2)}) %collective-permute-start.1) | collective-permute-done | bytes 65568 | tf_op jit(solution)/shard_map/ppermute | solution.py:267
  10.5 0.9 %normalize.1.normed_ref = bf16[64,1024]{1,0:T(8,128)(2,1)S(1)} custom-call(bf16[64,256]{1,0:T(8,128)(2,1)S(1)} %get-tuple-element.12.own_high, bf16[64,256]{1,0:T(8,128)(2,1)S(1)} %get-tuple-element.13.own_low, bf16[512,256]{1,0:T(8,128)(2,1)S(1)} %get-tuple-element.14.high_ref, bf16[512,256]{1,0:T(8,128)(2,1)S(1)} %get-tuple-element.15.low_ref, ...), custom_call_target="tpu_custom_call" | custom-call | tf_op jit(solution)/shard_map/normalize/pallas_call | solution.py:132
  11.4 1.6 %collective-permute-start.4 = (bf16[64,1024]{1,0:T(8,128)(2,1)S(1)}, bf16[64,1024]{1,0:T(8,128)(2,1)S(1)}, u32[]{:S(2)}, u32[]{:S(2)}) collective-permute-start(bf16[64,1024]{1,0:T(8,128)(2,1)S(1)} %normalize.1.normed_ref), channel_id=1, source_target_pairs={{0,2},{1,3},{2,0},{3,1},{4,6},{5,7},{6,4},{7,5},{8,10},{9,11},{10,... | collective-permute-start | bytes 393224 | tf_op jit(solution)/shard_map/ppermute | solution.py:270
  13.0 0.0 collective-permute-start.3
  13.0 3.4 %collective-permute-done.4.refs_1_ = bf16[64,1024]{1,0:T(8,128)(2,1)S(1)} collective-permute-done((bf16[64,1024]{1,0:T(8,128)(2,1)S(1)}, bf16[64,1024]{1,0:T(8,128)(2,1)S(1)}, u32[]{:S(2)}, u32[]{:S(2)}) %collective-permute-start.4) | collective-permute-done | bytes 131104 | tf_op jit(solution)/shard_map/ppermute | solution.py:270
  16.5 0.0 collective-permute-start.5
  16.5 0.7 %lags.1.lagged = bf16[1024,1152]{1,0:T(8,128)(2,1)S(1)} custom-call(bf16[64,1024]{1,0:T(8,128)(2,1)S(1)} %normalize.1.normed_ref), custom_call_target="tpu_custom_call" | custom-call | flops 2097152 | bytes 4194304 | tf_op jit(solution)/shard_map/lags/pallas_call | solution.py:159
  17.1 0.0 collective-permute-done.3.refs_0_
  17.2 0.6 %collective-permute-done.5.refs_2_ = bf16[64,1024]{1,0:T(8,128)(2,1)S(1)} collective-permute-done((bf16[64,1024]{1,0:T(8,128)(2,1)S(1)}, bf16[64,1024]{1,0:T(8,128)(2,1)S(1)}, u32[]{:S(2)}, u32[]{:S(2)}) %collective-permute-start.5) | collective-permute-done | bytes 131104 | tf_op jit(solution)/shard_map/ppermute | solution.py:270
  17.8 2.3 %correlate.1 = bf16[2,16,16448]{2,1,0:T(8,128)(2,1)} custom-call(bf16[2,64,128]{2,1,0:T(8,128)(2,1)S(1)} %get-tuple-element.11.picks_ref, bf16[1024,1152]{1,0:T(8,128)(2,1)S(1)} %lags.1.lagged, bf16[64,1024]{1,0:T(8,128)(2,1)S(1)} %collective-permute-done.3.refs_0_, bf16[64,1024]{1,0:T(8,128)(2,1)S(1)} %collective-permute-done.4.refs_1_, ...), custom_call_target="tpu_custom_call" | custom-call | tf_op jit(solution)/shard_map/correlate/pallas_call | solution.py:245
Async XLA Ops:
  0.0 8.7 %collective-permute-start = (f32[64,256]{1,0:T(8,128)}, f32[64,256]{1,0:T(8,128)S(1)}, u32[]{:S(2)}, u32[]{:S(2)}) collective-permute-start(f32[64,256]{1,0:T(8,128)} %param.3), channel_id=1, source_target_pairs={{0,4},{4,8},{8,12},{12,0},{1,5},{5,9},{9,13},{13,1},{2,6},{6,10},{... | collective-permute-start | bytes 196616 | tf_op jit(solution)/shard_map/ppermute | solution.py:267
  3.0 7.3 %collective-permute-start.2 = (f32[64,256]{1,0:T(8,128)}, f32[64,256]{1,0:T(8,128)S(1)}, u32[]{:S(2)}, u32[]{:S(2)}) collective-permute-start(f32[64,256]{1,0:T(8,128)} %param.3), channel_id=1, source_target_pairs={{0,8},{4,12},{8,0},{12,4},{1,9},{5,13},{9,1},{13,5},{2,10},{6,14},... | collective-permute-start | bytes 196616 | tf_op jit(solution)/shard_map/ppermute | solution.py:267
  5.6 4.9 %collective-permute-start.1 = (f32[64,256]{1,0:T(8,128)}, f32[64,256]{1,0:T(8,128)S(1)}, u32[]{:S(2)}, u32[]{:S(2)}) collective-permute-start(f32[64,256]{1,0:T(8,128)} %param.3), channel_id=1, source_target_pairs={{0,12},{4,0},{8,4},{12,8},{1,13},{5,1},{9,5},{13,9},{2,14},{6,2},{... | collective-permute-start | bytes 196616 | tf_op jit(solution)/shard_map/ppermute | solution.py:267
  11.4 5.1 %collective-permute-start.4 = (bf16[64,1024]{1,0:T(8,128)(2,1)S(1)}, bf16[64,1024]{1,0:T(8,128)(2,1)S(1)}, u32[]{:S(2)}, u32[]{:S(2)}) collective-permute-start(bf16[64,1024]{1,0:T(8,128)(2,1)S(1)} %normalize.1.normed_ref), channel_id=1, source_target_pairs={{0,2},{1,3},{2,0},{3,1},{4,6},{5,7},{6,4},{7,5},{8,10},{9,11},{10,... | collective-permute-start | bytes 393224 | tf_op jit(solution)/shard_map/ppermute | solution.py:270
  13.0 4.1 %collective-permute-start.3 = (bf16[64,1024]{1,0:T(8,128)(2,1)S(1)}, bf16[64,1024]{1,0:T(8,128)(2,1)S(1)}, u32[]{:S(2)}, u32[]{:S(2)}) collective-permute-start(bf16[64,1024]{1,0:T(8,128)(2,1)S(1)} %normalize.1.normed_ref), channel_id=1, source_target_pairs={{0,1},{1,0},{2,3},{3,2},{4,5},{5,4},{6,7},{7,6},{8,9},{9,8},{10,11... | collective-permute-start | bytes 393224 | tf_op jit(solution)/shard_map/ppermute | solution.py:270
  16.5 1.3 %collective-permute-start.5 = (bf16[64,1024]{1,0:T(8,128)(2,1)S(1)}, bf16[64,1024]{1,0:T(8,128)(2,1)S(1)}, u32[]{:S(2)}, u32[]{:S(2)}) collective-permute-start(bf16[64,1024]{1,0:T(8,128)(2,1)S(1)} %collective-permute-done.4.refs_1_), channel_id=1, source_target_pairs={{0,1},{1,0},{2,3},{3,2},{4,5},{5,4},{6,7},{7,6},{8,9},{9,8},{10,11... | collective-permute-start | bytes 393224 | tf_op jit(solution)/shard_map/ppermute | solution.py:270

commit v5 on v4

--- a/solution.py
+++ b/solution.py
@@ -18,6 +18,7 @@
 BLOCK = 256
 WINDOW = BLOCK + 2 * LANES
 TURNS = LANES // 2
+CHUNKS = 4
 MIB = 1024 * 1024
 
 VMEM = pl.BlockSpec(memory_space=pltpu.VMEM)
@@ -146,7 +147,7 @@
     own = jnp.concatenate([own, jnp.zeros((ROWS, LANES), jnp.float32)], axis=1)
     last = lax.broadcasted_iota(jnp.int32, (ROWS, LANES), 1) == LANES - 1
     samples = normed_ref.shape[1]
-    for turn in range(TURNS):
+    for turn in range(TURNS + 1):
         moved = pltpu.roll(own, 2 * turn, 1)
         tail = jnp.where(last, moved[:, :LANES], moved[:, samples:])
         at = slice(turn * ROWS, (turn + 1) * ROWS)
@@ -155,7 +156,7 @@
 
 
 def lags_of(normed, row_share):
-    shape = (TURNS * ROWS, normed.shape[1] + LANES)
+    shape = ((TURNS + 1) * ROWS, normed.shape[1] + LANES)
     return pl.pallas_call(
         functools.partial(lag_kernel, row_share),
         out_shape=jax.ShapeDtypeStruct(shape, jnp.bfloat16),
@@ -200,25 +201,19 @@
                 tile = jnp.where(slot == offset + 1.0, held, tile)
             tiles.append(tile)
         take(match, jnp.concatenate(tiles, axis=1))
-    lag_pairs = (LAGS + 1) // 2
-    per_chunk = 16
     copies = []
-    for wrap in range(-(-lag_pairs // TURNS)):
-        for chunk in range(TURNS // per_chunk):
-            steps = min(per_chunk, lag_pairs - wrap * TURNS - chunk * per_chunk)
-            if steps <= 0:
-                continue
-            begin = chunk * per_chunk * ROWS
-            skip = max(wrap - 1, 0) * LANES
-            first = LANES if wrap == 0 else 0
+    for wrap in range(2):
+        for chunk in range(CHUNKS):
+            begin = chunk * TURNS // CHUNKS
+            steps = TURNS // CHUNKS + (wrap == 1 and chunk == CHUNKS - 1)
             product = lax.dot_general(
-                lagged[begin : begin + steps * ROWS, first : first + samples - skip],
-                partner[min(wrap, 1), :, skip:],
+                lagged[begin * ROWS : (begin + steps) * ROWS, pl.ds((1 - wrap) * LANES, samples)],
+                partner[wrap],
                 (((1,), (1,)), ((), ())),
                 preferred_element_type=jnp.float32,
             )
             product = (product * scaling).astype(jnp.bfloat16)
-            left = (wrap * TURNS + chunk * per_chunk) * pair
+            left = (wrap * TURNS + begin) * pair
             for step in range(steps):
                 column = left + step * pair
                 width = min(pair, LAGS * group_ch - column)
@@ -250,7 +245,7 @@
         scratch_shapes=[
             pltpu.VMEM(partner, jnp.bfloat16),
             pltpu.VMEM(out, jnp.bfloat16),
-            pltpu.SemaphoreType.DMA((2 * (TURNS // ROWS) + 1,)),
+            pltpu.SemaphoreType.DMA((2 * CHUNKS,)),
         ],
         compiler_params=granted((lagged.shape, lagged.dtype), (out, jnp.bfloat16), *held),
         name="correlate",

time: 20.3 us -> 20.2 us (level)
  no operation moved by 1% of the time
where the time goes in v5:
time: 20.2 us; the launch traced here: 20 us
  starting transfers between devices  8.57 us (42%)
  waiting for transfers between devices  5.92 us (29%)
  Pallas kernels  3.93 us (19%)
  other arithmetic  1.54 us (8%)
    ppermute x3, starting transfers between devices, turned(): lax.ppermute(cells, axis, [(i, (i + step) % count) for i in range(count)])  6.96 us
    ppermute x3, waiting for transfers between devices, swapped(): lax.ppermute(cells, 'chan', [(i, i ^ bit) for i in range(group_count)])  4.1 us
    pallas_call x1, Pallas kernels, correlate(): pl.pallas_call(functools.partial(correlate_kernel, len(groups)), out_shap...  2.2 us
    ppermute x3, waiting for transfers between devices, turned(): lax.ppermute(cells, axis, [(i, (i + step) % count) for i in range(count)])  1.82 us
    ppermute x3, starting transfers between devices, swapped(): lax.ppermute(cells, 'chan', [(i, i ^ bit) for i in range(group_count)])  1.61 us
    add x1, other arithmetic, prepare(): placed(records, 0) + placed(fir_taps.reshape(1, -1), channels)  0.86 us
    pallas_call x1, Pallas kernels, normalize(): pl.pallas_call(functools.partial(normalize_kernel, steps), out_shape=jax....  0.86 us
    pallas_call x1, Pallas kernels, lags_of(): pl.pallas_call(functools.partial(lag_kernel, row_share), out_shape=jax.Sh...  0.68 us
  transfers between devices with their start and end apart: 6, of which 4 were waited for; matrix products, arithmetic and copies ran while one was open for 8% of the time, Pallas kernels for 4%

profile of v5, /device:TPU:0, one launch (start us, length us, event | category | flops | bytes accessed | tf_op | source)
XLA Modules:
  0.0 20.0 jit_solution(14424650963644336259)
XLA Ops:
  0.0 3.0 %collective-permute-start = (f32[64,256]{1,0:T(8,128)}, f32[64,256]{1,0:T(8,128)S(1)}, u32[]{:S(2)}, u32[]{:S(2)}) collective-permute-start(f32[64,256]{1,0:T(8,128)} %param.3), channel_id=1, source_target_pairs={{0,4},{4,8},{8,12},{12,0},{1,5},{5,9},{9,13},{13,1},{2,6},{6,10},{... | collective-permute-start | bytes 196616 | tf_op jit(solution)/shard_map/ppermute | solution.py:262
  3.0 2.6 %collective-permute-start.2 = (f32[64,256]{1,0:T(8,128)}, f32[64,256]{1,0:T(8,128)S(1)}, u32[]{:S(2)}, u32[]{:S(2)}) collective-permute-start(f32[64,256]{1,0:T(8,128)} %param.3), channel_id=1, source_target_pairs={{0,8},{4,12},{8,0},{12,4},{1,9},{5,13},{9,1},{13,5},{2,10},{6,14},... | collective-permute-start | bytes 196616 | tf_op jit(solution)/shard_map/ppermute | solution.py:262
  5.6 1.3 %collective-permute-start.1 = (f32[64,256]{1,0:T(8,128)}, f32[64,256]{1,0:T(8,128)S(1)}, u32[]{:S(2)}, u32[]{:S(2)}) collective-permute-start(f32[64,256]{1,0:T(8,128)} %param.3), channel_id=1, source_target_pairs={{0,12},{4,0},{8,4},{12,8},{1,13},{5,1},{9,5},{13,9},{2,14},{6,2},{... | collective-permute-start | bytes 196616 | tf_op jit(solution)/shard_map/ppermute | solution.py:262
  7.0 0.7 %convert_element_type.9 = f32[2,4]{1,0:T(2,128)S(1)} convert(s32[2,4]{1,0:T(2,128)} %param.5) | non-fusion elementwise | flops 8 | bytes 64 | tf_op jit(solution)/shard_map/convert_element_type | solution.py:76
  7.6 0.9 %pad_add_fusion.packed_ref = f32[72,256]{1,0:T(8,128)S(1)} fusion(f32[2,4]{1,0:T(2,128)S(1)} %convert_element_type.9, f32[1,129]{1,0:T(1,128)} %bitcast.4, f32[64,256]{1,0:T(8,128)} %param.3), kind=kLoop, calls=%fused_computation | loop fusion | flops 36864 | bytes 139812 | tf_op jit(solution)/shard_map/add | solution.py:74
  8.5 0.2 prepare.1
  8.7 0.0 collective-permute-done.refs_0_
  8.7 1.6 %collective-permute-done.2.refs_2_ = f32[64,256]{1,0:T(8,128)S(1)} collective-permute-done((f32[64,256]{1,0:T(8,128)}, f32[64,256]{1,0:T(8,128)S(1)}, u32[]{:S(2)}, u32[]{:S(2)}) %collective-permute-start.2) | collective-permute-done | bytes 65568 | tf_op jit(solution)/shard_map/ppermute | solution.py:262
  10.3 0.2 %collective-permute-done.1.refs_1_ = f32[64,256]{1,0:T(8,128)S(1)} collective-permute-done((f32[64,256]{1,0:T(8,128)}, f32[64,256]{1,0:T(8,128)S(1)}, u32[]{:S(2)}, u32[]{:S(2)}) %collective-permute-start.1) | collective-permute-done | bytes 65568 | tf_op jit(solution)/shard_map/ppermute | solution.py:262
  10.5 0.9 %normalize.1.normed_ref = bf16[64,1024]{1,0:T(8,128)(2,1)S(1)} custom-call(bf16[64,256]{1,0:T(8,128)(2,1)S(1)} %get-tuple-element.12.own_high, bf16[64,256]{1,0:T(8,128)(2,1)S(1)} %get-tuple-element.13.own_low, bf16[512,256]{1,0:T(8,128)(2,1)S(1)} %get-tuple-element.14.high_ref, bf16[512,256]{1,0:T(8,128)(2,1)S(1)} %get-tuple-element.15.low_ref, ...), custom_call_target="tpu_custom_call" | custom-call | tf_op jit(solution)/shard_map/normalize/pallas_call | solution.py:133
  11.4 1.6 %collective-permute-start.4 = (bf16[64,1024]{1,0:T(8,128)(2,1)S(1)}, bf16[64,1024]{1,0:T(8,128)(2,1)S(1)}, u32[]{:S(2)}, u32[]{:S(2)}) collective-permute-start(bf16[64,1024]{1,0:T(8,128)(2,1)S(1)} %normalize.1.normed_ref), channel_id=1, source_target_pairs={{0,2},{1,3},{2,0},{3,1},{4,6},{5,7},{6,4},{7,5},{8,10},{9,11},{10,... | collective-permute-start | bytes 393224 | tf_op jit(solution)/shard_map/ppermute | solution.py:265
  13.0 0.0 collective-permute-start.3
  13.0 3.4 %collective-permute-done.4.refs_1_ = bf16[64,1024]{1,0:T(8,128)(2,1)S(1)} collective-permute-done((bf16[64,1024]{1,0:T(8,128)(2,1)S(1)}, bf16[64,1024]{1,0:T(8,128)(2,1)S(1)}, u32[]{:S(2)}, u32[]{:S(2)}) %collective-permute-start.4) | collective-permute-done | bytes 131104 | tf_op jit(solution)/shard_map/ppermute | solution.py:265
  16.5 0.0 collective-permute-start.5
  16.5 0.7 %lags.1.lagged = bf16[1040,1152]{1,0:T(8,128)(2,1)S(1)} custom-call(bf16[64,1024]{1,0:T(8,128)(2,1)S(1)} %normalize.1.normed_ref), custom_call_target="tpu_custom_call" | custom-call | flops 2097152 | bytes 4194304 | tf_op jit(solution)/shard_map/lags/pallas_call | solution.py:160
  17.1 0.0 collective-permute-done.3.refs_0_
  17.2 0.6 %collective-permute-done.5.refs_2_ = bf16[64,1024]{1,0:T(8,128)(2,1)S(1)} collective-permute-done((bf16[64,1024]{1,0:T(8,128)(2,1)S(1)}, bf16[64,1024]{1,0:T(8,128)(2,1)S(1)}, u32[]{:S(2)}, u32[]{:S(2)}) %collective-permute-start.5) | collective-permute-done | bytes 131104 | tf_op jit(solution)/shard_map/ppermute | solution.py:265
  17.8 2.2 %correlate.1 = bf16[2,16,16448]{2,1,0:T(8,128)(2,1)} custom-call(bf16[2,64,128]{2,1,0:T(8,128)(2,1)S(1)} %get-tuple-element.11.picks_ref, bf16[1040,1152]{1,0:T(8,128)(2,1)S(1)} %lags.1.lagged, bf16[64,1024]{1,0:T(8,128)(2,1)S(1)} %collective-permute-done.3.refs_0_, bf16[64,1024]{1,0:T(8,128)(2,1)S(1)} %collective-permute-done.4.refs_1_, ...), custom_call_target="tpu_custom_call" | custom-call | tf_op jit(solution)/shard_map/correlate/pallas_call | solution.py:240
Async XLA Ops:
  0.0 8.7 %collective-permute-start = (f32[64,256]{1,0:T(8,128)}, f32[64,256]{1,0:T(8,128)S(1)}, u32[]{:S(2)}, u32[]{:S(2)}) collective-permute-start(f32[64,256]{1,0:T(8,128)} %param.3), channel_id=1, source_target_pairs={{0,4},{4,8},{8,12},{12,0},{1,5},{5,9},{9,13},{13,1},{2,6},{6,10},{... | collective-permute-start | bytes 196616 | tf_op jit(solution)/shard_map/ppermute | solution.py:262
  3.0 7.3 %collective-permute-start.2 = (f32[64,256]{1,0:T(8,128)}, f32[64,256]{1,0:T(8,128)S(1)}, u32[]{:S(2)}, u32[]{:S(2)}) collective-permute-start(f32[64,256]{1,0:T(8,128)} %param.3), channel_id=1, source_target_pairs={{0,8},{4,12},{8,0},{12,4},{1,9},{5,13},{9,1},{13,5},{2,10},{6,14},... | collective-permute-start | bytes 196616 | tf_op jit(solution)/shard_map/ppermute | solution.py:262
  5.6 4.9 %collective-permute-start.1 = (f32[64,256]{1,0:T(8,128)}, f32[64,256]{1,0:T(8,128)S(1)}, u32[]{:S(2)}, u32[]{:S(2)}) collective-permute-start(f32[64,256]{1,0:T(8,128)} %param.3), channel_id=1, source_target_pairs={{0,12},{4,0},{8,4},{12,8},{1,13},{5,1},{9,5},{13,9},{2,14},{6,2},{... | collective-permute-start | bytes 196616 | tf_op jit(solution)/shard_map/ppermute | solution.py:262
  11.4 5.1 %collective-permute-start.4 = (bf16[64,1024]{1,0:T(8,128)(2,1)S(1)}, bf16[64,1024]{1,0:T(8,128)(2,1)S(1)}, u32[]{:S(2)}, u32[]{:S(2)}) collective-permute-start(bf16[64,1024]{1,0:T(8,128)(2,1)S(1)} %normalize.1.normed_ref), channel_id=1, source_target_pairs={{0,2},{1,3},{2,0},{3,1},{4,6},{5,7},{6,4},{7,5},{8,10},{9,11},{10,... | collective-permute-start | bytes 393224 | tf_op jit(solution)/shard_map/ppermute | solution.py:265
  13.0 4.1 %collective-permute-start.3 = (bf16[64,1024]{1,0:T(8,128)(2,1)S(1)}, bf16[64,1024]{1,0:T(8,128)(2,1)S(1)}, u32[]{:S(2)}, u32[]{:S(2)}) collective-permute-start(bf16[64,1024]{1,0:T(8,128)(2,1)S(1)} %normalize.1.normed_ref), channel_id=1, source_target_pairs={{0,1},{1,0},{2,3},{3,2},{4,5},{5,4},{6,7},{7,6},{8,9},{9,8},{10,11... | collective-permute-start | bytes 393224 | tf_op jit(solution)/shard_map/ppermute | solution.py:265
  16.5 1.3 %collective-permute-start.5 = (bf16[64,1024]{1,0:T(8,128)(2,1)S(1)}, bf16[64,1024]{1,0:T(8,128)(2,1)S(1)}, u32[]{:S(2)}, u32[]{:S(2)}) collective-permute-start(bf16[64,1024]{1,0:T(8,128)(2,1)S(1)} %collective-permute-done.4.refs_1_), channel_id=1, source_target_pairs={{0,1},{1,0},{2,3},{3,2},{4,5},{5,4},{6,7},{7,6},{8,9},{9,8},{10,11... | collective-permute-start | bytes 393224 | tf_op jit(solution)/shard_map/ppermute | solution.py:265

commit v6 on v5

--- a/solution.py
+++ b/solution.py
@@ -15,8 +15,8 @@
 
 LANES = 128
 ROWS = 16
-BLOCK = 256
-WINDOW = BLOCK + 2 * LANES
+HALF = LANES // 2
+WINDOW = 2 * LANES
 TURNS = LANES // 2
 CHUNKS = 4
 MIB = 1024 * 1024
@@ -40,18 +40,18 @@
 
 
 def prepare_kernel(match_count, taps, packed_ref, *refs):
-    high_ref, low_ref, band_ref, own_high_ref, own_low_ref, slots_ref, row = refs
+    bands_ref, near_ref, own_high_ref, own_low_ref, slots_ref, row = refs
     channels = own_high_ref.shape[0]
     row[...] = jnp.zeros_like(row)
     row[0:1, 0:taps] = packed_ref[channels : channels + 1, 0:taps]
-    spread = jnp.broadcast_to(row[0:1, :], (WINDOW, WINDOW))
-    shift = (taps // 2 - LANES - taps + 1) % WINDOW
-    banded = pltpu.roll(spread, shift, 1, stride=1, stride_axis=0)[:, :BLOCK]
-    high_ref[...], low_ref[...] = split(banded)
-    rows_at = lax.broadcasted_iota(jnp.int32, (WINDOW, BLOCK), 0) - LANES
-    cols_at = lax.broadcasted_iota(jnp.int32, (WINDOW, BLOCK), 1)
+    spread = jnp.broadcast_to(row[0:1, :], (WINDOW, 2 * WINDOW))
+    shift = 2 * WINDOW - HALF - taps // 2
+    banded = pltpu.roll(spread, shift, 1, stride=1, stride_axis=0)[:, :LANES]
+    bands_ref[:, :LANES], bands_ref[:, LANES:] = split(banded)
+    rows_at = lax.broadcasted_iota(jnp.int32, (WINDOW, LANES), 0) - HALF
+    cols_at = lax.broadcasted_iota(jnp.int32, (WINDOW, LANES), 1)
     near = jnp.abs(rows_at - cols_at) <= AVG // 2
-    band_ref[...] = near.astype(jnp.float32).astype(jnp.bfloat16)
+    near_ref[...] = near.astype(jnp.float32).astype(jnp.bfloat16)
     own_high_ref[...], own_low_ref[...] = split(packed_ref[:channels, :])
     group = lax.axis_index("chan")
     here = lax.broadcasted_iota(jnp.int32, (1, LANES), 1) == group
@@ -75,23 +75,24 @@
         + placed(fir_taps.reshape(1, -1), channels)
         + placed(matchings.astype(jnp.float32), channels + 1)
     )
-    banded = jax.ShapeDtypeStruct((WINDOW, BLOCK), jnp.bfloat16)
+    bands = jax.ShapeDtypeStruct((WINDOW, 2 * LANES), jnp.bfloat16)
+    near = jax.ShapeDtypeStruct((WINDOW, LANES), jnp.bfloat16)
     own = jax.ShapeDtypeStruct(records.shape, jnp.bfloat16)
     slots = jax.ShapeDtypeStruct((match_count, channels, LANES), jnp.bfloat16)
-    outs = (banded,) * 3 + (own,) * 2 + (slots,)
+    outs = (bands, near, own, own, slots)
     return pl.pallas_call(
         functools.partial(prepare_kernel, match_count, taps),
         out_shape=outs,
         in_specs=[VMEM],
         out_specs=(VMEM,) * len(outs),
-        scratch_shapes=[pltpu.VMEM((8, WINDOW), jnp.float32)],
+        scratch_shapes=[pltpu.VMEM((8, 2 * WINDOW), jnp.float32)],
         compiler_params=granted(((WINDOW, 4 * WINDOW), jnp.float32)),
         cost_estimate=pl.CostEstimate(flops=2 * MIB, bytes_accessed=MIB, transcendentals=0),
         name="prepare",
     )(packed)
 
 
-def normalize_kernel(steps, own_high, own_low, high_ref, low_ref, band_ref, *refs):
+def normalize_kernel(steps, own_high, own_low, bands_ref, near_ref, *refs):
     blocks, (out_ref, high, low) = refs[:-3], refs[-3:]
     channels, samples_dev = own_high.shape
     count = len(blocks) + 1
@@ -108,22 +109,35 @@
             high[:, at], low[:, at] = own_high[...], own_low[...]
         else:
             high[:, at], low[:, at] = split(block[...])
-    parts = samples // BLOCK
-
-    def windows(part):
+    tiles = samples // LANES
+
+    def windows(part, count):
         return jnp.concatenate(
-            [part[:, n * BLOCK : n * BLOCK + WINDOW] for n in range(parts)], axis=0
+            [part[:, n * LANES : n * LANES + WINDOW] for n in range(count)], axis=0
         )
 
-    highs, lows = windows(high), windows(low)
-    filtered = mm(highs, high_ref[...]) + (mm(highs, low_ref[...]) + mm(lows, high_ref[...]))
-    for n in range(parts):
-        at = slice(LANES + n * BLOCK, LANES + (n + 1) * BLOCK)
-        high[:, at], low[:, at] = split(jnp.abs(filtered[n * channels : (n + 1) * channels]))
-    local_mean = (mm(windows(high), band_ref[...]) + mm(windows(low), band_ref[...])) * (1.0 / AVG)
-    normed = (filtered / (local_mean + EPSILON)).astype(jnp.bfloat16)
-    for n in range(parts):
-        out_ref[:, n * BLOCK : (n + 1) * BLOCK] = normed[n * channels : (n + 1) * channels]
+    product = mm(windows(high, tiles + 1), bands_ref[...])
+    product = product[:, :LANES] + (
+        product[:, LANES:] + mm(windows(low, tiles + 1), bands_ref[:, :LANES])
+    )
+    early = lax.broadcasted_iota(jnp.int32, (channels, LANES), 1) < HALF
+    turned = []
+    for n in range(tiles + 1):
+        filtered = product[n * channels : (n + 1) * channels]
+        if n == 0:
+            filtered = jnp.where(early, 0.0, filtered)
+        if n == tiles:
+            filtered = jnp.where(early, filtered, 0.0)
+        at = slice(n * LANES, (n + 1) * LANES)
+        high[:, at], low[:, at] = split(jnp.abs(filtered))
+        turned.append(pltpu.roll(filtered, HALF, 1))
+    sums = mm(windows(high, tiles), near_ref[...]) + mm(windows(low, tiles), near_ref[...])
+    for n in range(tiles):
+        filtered = jnp.where(early, turned[n], turned[n + 1])
+        local_mean = sums[n * channels : (n + 1) * channels] * (1.0 / AVG)
+        out_ref[:, n * LANES : (n + 1) * LANES] = (filtered / (local_mean + EPSILON)).astype(
+            jnp.bfloat16
+        )
 
 
 def normalize(own, banded, steps, blocks):
@@ -133,7 +147,7 @@
     return pl.pallas_call(
         functools.partial(normalize_kernel, steps),
         out_shape=jax.ShapeDtypeStruct((channels, samples), jnp.bfloat16),
-        in_specs=[VMEM] * (len(blocks) + 5),
+        in_specs=[VMEM] * (len(blocks) + 4),
         out_specs=VMEM,
         scratch_shapes=[pltpu.VMEM(padded, jnp.bfloat16)] * 2,
         compiler_params=granted((padded, jnp.float32), (padded, jnp.float32)),
@@ -202,7 +216,7 @@
             tiles.append(tile)
         take(match, jnp.concatenate(tiles, axis=1))
     copies = []
-    for wrap in range(2):
+    for wrap in (1, 0):
         for chunk in range(CHUNKS):
             begin = chunk * TURNS // CHUNKS
             steps = TURNS // CHUNKS + (wrap == 1 and chunk == CHUNKS - 1)

time: 20.2 us -> 19.8 us (0.980)
  Pallas kernels: 3.93 us -> 3.54 us
    pallas_call x1, Pallas kernels: 0.86 us -> 0.52 us  [normalize(): pl.pallas_call(functools.partial(normalize_kernel, steps), out_shape=jax....]
where the time goes in v6:
time: 19.8 us; the launch traced here: 19.7 us
  starting transfers between devices  8.57 us (43%)
  waiting for transfers between devices  5.96 us (30%)
  Pallas kernels  3.54 us (18%)
  other arithmetic  1.54 us (8%)
    ppermute x3, starting transfers between devices, turned(): lax.ppermute(cells, axis, [(i, (i + step) % count) for i in range(count)])  6.96 us
    ppermute x3, waiting for transfers between devices, swapped(): lax.ppermute(cells, 'chan', [(i, i ^ bit) for i in range(group_count)])  4.09 us
    pallas_call x1, Pallas kernels, correlate(): pl.pallas_call(functools.partial(correlate_kernel, len(groups)), out_shap...  2.19 us
    ppermute x3, waiting for transfers between devices, turned(): lax.ppermute(cells, axis, [(i, (i + step) % count) for i in range(count)])  1.86 us
    ppermute x3, starting transfers between devices, swapped(): lax.ppermute(cells, 'chan', [(i, i ^ bit) for i in range(group_count)])  1.61 us
    add x1, other arithmetic, prepare(): placed(records, 0) + placed(fir_taps.reshape(1, -1), channels)  0.86 us
    pallas_call x1, Pallas kernels, lags_of(): pl.pallas_call(functools.partial(lag_kernel, row_share), out_shape=jax.Sh...  0.68 us
    convert_element_type x1, other arithmetic, prepare(): matchings.astype(jnp.float32)  0.68 us
  transfers between devices with their start and end apart: 6, of which 4 were waited for; matrix products, arithmetic and copies ran while one was open for 8% of the time, Pallas kernels for 4%

profile of v6, /device:TPU:0, one launch (start us, length us, event | category | flops | bytes accessed | tf_op | source)
XLA Modules:
  0.0 19.7 jit_solution(4477342678490643955)
XLA Ops:
  0.0 3.0 %collective-permute-start = (f32[64,256]{1,0:T(8,128)}, f32[64,256]{1,0:T(8,128)S(1)}, u32[]{:S(2)}, u32[]{:S(2)}) collective-permute-start(f32[64,256]{1,0:T(8,128)} %param.3), channel_id=1, source_target_pairs={{0,4},{4,8},{8,12},{12,0},{1,5},{5,9},{9,13},{13,1},{2,6},{6,10},{... | collective-permute-start | bytes 196616 | tf_op jit(solution)/shard_map/ppermute | solution.py:276
  3.0 2.6 %collective-permute-start.2 = (f32[64,256]{1,0:T(8,128)}, f32[64,256]{1,0:T(8,128)S(1)}, u32[]{:S(2)}, u32[]{:S(2)}) collective-permute-start(f32[64,256]{1,0:T(8,128)} %param.3), channel_id=1, source_target_pairs={{0,8},{4,12},{8,0},{12,4},{1,9},{5,13},{9,1},{13,5},{2,10},{6,14},... | collective-permute-start | bytes 196616 | tf_op jit(solution)/shard_map/ppermute | solution.py:276
  5.6 1.3 %collective-permute-start.1 = (f32[64,256]{1,0:T(8,128)}, f32[64,256]{1,0:T(8,128)S(1)}, u32[]{:S(2)}, u32[]{:S(2)}) collective-permute-start(f32[64,256]{1,0:T(8,128)} %param.3), channel_id=1, source_target_pairs={{0,12},{4,0},{8,4},{12,8},{1,13},{5,1},{9,5},{13,9},{2,14},{6,2},{... | collective-permute-start | bytes 196616 | tf_op jit(solution)/shard_map/ppermute | solution.py:276
  7.0 0.7 %convert_element_type.9 = f32[2,4]{1,0:T(2,128)S(1)} convert(s32[2,4]{1,0:T(2,128)} %param.5) | non-fusion elementwise | flops 8 | bytes 64 | tf_op jit(solution)/shard_map/convert_element_type | solution.py:76
  7.6 0.9 %pad_add_fusion.packed_ref = f32[72,256]{1,0:T(8,128)S(1)} fusion(f32[2,4]{1,0:T(2,128)S(1)} %convert_element_type.9, f32[1,129]{1,0:T(1,128)} %bitcast.4, f32[64,256]{1,0:T(8,128)} %param.3), kind=kLoop, calls=%fused_computation | loop fusion | flops 36864 | bytes 139812 | tf_op jit(solution)/shard_map/add | solution.py:74
  8.5 0.2 prepare.1
  8.7 0.0 collective-permute-done.refs_0_
  8.7 1.6 %collective-permute-done.2.refs_2_ = f32[64,256]{1,0:T(8,128)S(1)} collective-permute-done((f32[64,256]{1,0:T(8,128)}, f32[64,256]{1,0:T(8,128)S(1)}, u32[]{:S(2)}, u32[]{:S(2)}) %collective-permute-start.2) | collective-permute-done | bytes 65568 | tf_op jit(solution)/shard_map/ppermute | solution.py:276
  10.3 0.2 %collective-permute-done.1.refs_1_ = f32[64,256]{1,0:T(8,128)S(1)} collective-permute-done((f32[64,256]{1,0:T(8,128)}, f32[64,256]{1,0:T(8,128)S(1)}, u32[]{:S(2)}, u32[]{:S(2)}) %collective-permute-start.1) | collective-permute-done | bytes 65568 | tf_op jit(solution)/shard_map/ppermute | solution.py:276
  10.5 0.5 %normalize.1.normed_ref = bf16[64,1024]{1,0:T(8,128)(2,1)S(1)} custom-call(bf16[64,256]{1,0:T(8,128)(2,1)S(1)} %get-tuple-element.11.own_high, bf16[64,256]{1,0:T(8,128)(2,1)S(1)} %get-tuple-element.12.own_low, bf16[256,256]{1,0:T(8,128)(2,1)S(1)} %get-tuple-element.13.bands_ref, bf16[256,128]{1,0:T(8,128)(2,1)S(1)} %get-tuple-element.14.near_ref, ...), custom_call_target="tpu_custom_call" | custom-call | tf_op jit(solution)/shard_map/normalize/pallas_call | solution.py:147
  11.1 1.6 %collective-permute-start.4 = (bf16[64,1024]{1,0:T(8,128)(2,1)S(1)}, bf16[64,1024]{1,0:T(8,128)(2,1)S(1)}, u32[]{:S(2)}, u32[]{:S(2)}) collective-permute-start(bf16[64,1024]{1,0:T(8,128)(2,1)S(1)} %normalize.1.normed_ref), channel_id=1, source_target_pairs={{0,2},{1,3},{2,0},{3,1},{4,6},{5,7},{6,4},{7,5},{8,10},{9,11},{10,... | collective-permute-start | bytes 393224 | tf_op jit(solution)/shard_map/ppermute | solution.py:279
  12.7 0.0 collective-permute-start.3
  12.7 3.4 %collective-permute-done.4.refs_1_ = bf16[64,1024]{1,0:T(8,128)(2,1)S(1)} collective-permute-done((bf16[64,1024]{1,0:T(8,128)(2,1)S(1)}, bf16[64,1024]{1,0:T(8,128)(2,1)S(1)}, u32[]{:S(2)}, u32[]{:S(2)}) %collective-permute-start.4) | collective-permute-done | bytes 131104 | tf_op jit(solution)/shard_map/ppermute | solution.py:279
  16.1 0.0 collective-permute-start.5
  16.1 0.7 %lags.1.lagged = bf16[1040,1152]{1,0:T(8,128)(2,1)S(1)} custom-call(bf16[64,1024]{1,0:T(8,128)(2,1)S(1)} %normalize.1.normed_ref), custom_call_target="tpu_custom_call" | custom-call | flops 2097152 | bytes 4194304 | tf_op jit(solution)/shard_map/lags/pallas_call | solution.py:174
  16.8 0.0 collective-permute-done.3.refs_0_
  16.8 0.6 %collective-permute-done.5.refs_2_ = bf16[64,1024]{1,0:T(8,128)(2,1)S(1)} collective-permute-done((bf16[64,1024]{1,0:T(8,128)(2,1)S(1)}, bf16[64,1024]{1,0:T(8,128)(2,1)S(1)}, u32[]{:S(2)}, u32[]{:S(2)}) %collective-permute-start.5) | collective-permute-done | bytes 131104 | tf_op jit(solution)/shard_map/ppermute | solution.py:279
  17.5 2.2 %correlate.1 = bf16[2,16,16448]{2,1,0:T(8,128)(2,1)} custom-call(bf16[2,64,128]{2,1,0:T(8,128)(2,1)S(1)} %get-tuple-element.10.picks_ref, bf16[1040,1152]{1,0:T(8,128)(2,1)S(1)} %lags.1.lagged, bf16[64,1024]{1,0:T(8,128)(2,1)S(1)} %collective-permute-done.3.refs_0_, bf16[64,1024]{1,0:T(8,128)(2,1)S(1)} %collective-permute-done.4.refs_1_, ...), custom_call_target="tpu_custom_call" | custom-call | tf_op jit(solution)/shard_map/correlate/pallas_call | solution.py:254
Async XLA Ops:
  0.0 8.7 %collective-permute-start = (f32[64,256]{1,0:T(8,128)}, f32[64,256]{1,0:T(8,128)S(1)}, u32[]{:S(2)}, u32[]{:S(2)}) collective-permute-start(f32[64,256]{1,0:T(8,128)} %param.3), channel_id=1, source_target_pairs={{0,4},{4,8},{8,12},{12,0},{1,5},{5,9},{9,13},{13,1},{2,6},{6,10},{... | collective-permute-start | bytes 196616 | tf_op jit(solution)/shard_map/ppermute | solution.py:276
  3.0 7.3 %collective-permute-start.2 = (f32[64,256]{1,0:T(8,128)}, f32[64,256]{1,0:T(8,128)S(1)}, u32[]{:S(2)}, u32[]{:S(2)}) collective-permute-start(f32[64,256]{1,0:T(8,128)} %param.3), channel_id=1, source_target_pairs={{0,8},{4,12},{8,0},{12,4},{1,9},{5,13},{9,1},{13,5},{2,10},{6,14},... | collective-permute-start | bytes 196616 | tf_op jit(solution)/shard_map/ppermute | solution.py:276
  5.6 4.9 %collective-permute-start.1 = (f32[64,256]{1,0:T(8,128)}, f32[64,256]{1,0:T(8,128)S(1)}, u32[]{:S(2)}, u32[]{:S(2)}) collective-permute-start(f32[64,256]{1,0:T(8,128)} %param.3), channel_id=1, source_target_pairs={{0,12},{4,0},{8,4},{12,8},{1,13},{5,1},{9,5},{13,9},{2,14},{6,2},{... | collective-permute-start | bytes 196616 | tf_op jit(solution)/shard_map/ppermute | solution.py:276
  11.1 5.1 %collective-permute-start.4 = (bf16[64,1024]{1,0:T(8,128)(2,1)S(1)}, bf16[64,1024]{1,0:T(8,128)(2,1)S(1)}, u32[]{:S(2)}, u32[]{:S(2)}) collective-permute-start(bf16[64,1024]{1,0:T(8,128)(2,1)S(1)} %normalize.1.normed_ref), channel_id=1, source_target_pairs={{0,2},{1,3},{2,0},{3,1},{4,6},{5,7},{6,4},{7,5},{8,10},{9,11},{10,... | collective-permute-start | bytes 393224 | tf_op jit(solution)/shard_map/ppermute | solution.py:279
  12.7 4.1 %collective-permute-start.3 = (bf16[64,1024]{1,0:T(8,128)(2,1)S(1)}, bf16[64,1024]{1,0:T(8,128)(2,1)S(1)}, u32[]{:S(2)}, u32[]{:S(2)}) collective-permute-start(bf16[64,1024]{1,0:T(8,128)(2,1)S(1)} %normalize.1.normed_ref), channel_id=1, source_target_pairs={{0,1},{1,0},{2,3},{3,2},{4,5},{5,4},{6,7},{7,6},{8,9},{9,8},{10,11... | collective-permute-start | bytes 393224 | tf_op jit(solution)/shard_map/ppermute | solution.py:279
  16.1 1.3 %collective-permute-start.5 = (bf16[64,1024]{1,0:T(8,128)(2,1)S(1)}, bf16[64,1024]{1,0:T(8,128)(2,1)S(1)}, u32[]{:S(2)}, u32[]{:S(2)}) collective-permute-start(bf16[64,1024]{1,0:T(8,128)(2,1)S(1)} %collective-permute-done.4.refs_1_), channel_id=1, source_target_pairs={{0,1},{1,0},{2,3},{3,2},{4,5},{5,4},{6,7},{7,6},{8,9},{9,8},{10,11... | collective-permute-start | bytes 393224 | tf_op jit(solution)/shard_map/ppermute | solution.py:279

commit v7 on v6

--- a/solution.py
+++ b/solution.py
@@ -183,7 +183,7 @@
 
 
 def correlate_kernel(parcels, picks_ref, lagged, *refs):
-    groups, (out_ref, partner, result, sem) = refs[:parcels], refs[parcels:]
+    groups, (out_ref, partner, first_end, result, sem) = refs[:parcels], refs[parcels:]
     match_count = picks_ref.shape[0]
     group_ch, samples = groups[0].shape[-2:]
     scaling = 1.0 / math.sqrt(samples)
@@ -193,14 +193,12 @@
     def take(match, rows):
         even, odd = pl.ds(match * pair, group_ch), pl.ds(match * pair + group_ch, group_ch)
         ahead = pltpu.roll(rows.astype(jnp.float32), samples - 1, 1)
-        body, end = slice(0, samples - LANES), slice(samples - LANES, samples)
-        for wrap in range(2):
-            partner[wrap, even, body] = rows[:, body].astype(jnp.bfloat16)
-            partner[wrap, odd, body] = ahead[:, body].astype(jnp.bfloat16)
-        partner[1, even, end] = rows[:, end].astype(jnp.bfloat16)
-        partner[0, odd, end] = ahead[:, end].astype(jnp.bfloat16)
-        partner[0, even, end] = jnp.where(last, 0.0, rows[:, end].astype(jnp.float32)).astype(jnp.bfloat16)
-        partner[1, odd, end] = jnp.where(last, 0.0, ahead[:, end]).astype(jnp.bfloat16)
+        end = slice(samples - LANES, samples)
+        partner[even, :] = rows.astype(jnp.bfloat16)
+        partner[odd, : samples - LANES] = ahead[:, : samples - LANES].astype(jnp.bfloat16)
+        partner[odd, end] = jnp.where(last, 0.0, ahead[:, end]).astype(jnp.bfloat16)
+        first_end[even, :] = jnp.where(last, 0.0, rows[:, end].astype(jnp.float32)).astype(jnp.bfloat16)
+        first_end[odd, :] = ahead[:, end].astype(jnp.bfloat16)
 
     for match in range(match_count):
         if parcels == 1:
@@ -217,12 +215,14 @@
         take(match, jnp.concatenate(tiles, axis=1))
     copies = []
     for wrap in (1, 0):
+        if wrap == 0:
+            partner[:, samples - LANES :] = first_end[...]
         for chunk in range(CHUNKS):
             begin = chunk * TURNS // CHUNKS
             steps = TURNS // CHUNKS + (wrap == 1 and chunk == CHUNKS - 1)
             product = lax.dot_general(
                 lagged[begin * ROWS : (begin + steps) * ROWS, pl.ds((1 - wrap) * LANES, samples)],
-                partner[wrap],
+                partner[...],
                 (((1,), (1,)), ((), ())),
                 preferred_element_type=jnp.float32,
             )
@@ -249,7 +249,7 @@
     match_count = picks.shape[0]
     group_ch, samples = groups[0].shape[-2:]
     out = (match_count, ROWS, LAGS * group_ch)
-    partner = (2, 2 * match_count * group_ch, samples)
+    partner = (2 * match_count * group_ch, samples)
     held = [(g.shape, g.dtype) for g in groups]
     return pl.pallas_call(
         functools.partial(correlate_kernel, len(groups)),
@@ -258,6 +258,7 @@
         out_specs=pl.BlockSpec(memory_space=pl.ANY),
         scratch_shapes=[
             pltpu.VMEM(partner, jnp.bfloat16),
+            pltpu.VMEM((partner[0], LANES), jnp.bfloat16),
             pltpu.VMEM(out, jnp.bfloat16),
             pltpu.SemaphoreType.DMA((2 * CHUNKS,)),
         ],

time: 19.8 us -> 19.8 us (level)
  no operation moved by 1% of the time
where the time goes in v7:
time: 19.8 us; the launch traced here: 19.7 us
  starting transfers between devices  8.57 us (43%)
  waiting for transfers between devices  5.96 us (30%)
  Pallas kernels  3.54 us (18%)
  other arithmetic  1.54 us (8%)
    ppermute x3, starting transfers between devices, turned(): lax.ppermute(cells, axis, [(i, (i + step) % count) for i in range(count)])  6.96 us
    ppermute x3, waiting for transfers between devices, swapped(): lax.ppermute(cells, 'chan', [(i, i ^ bit) for i in range(group_count)])  4.09 us
    pallas_call x1, Pallas kernels, correlate(): pl.pallas_call(functools.partial(correlate_kernel, len(groups)), out_shap...  2.19 us
    ppermute x3, waiting for transfers between devices, turned(): lax.ppermute(cells, axis, [(i, (i + step) % count) for i in range(count)])  1.86 us
    ppermute x3, starting transfers between devices, swapped(): lax.ppermute(cells, 'chan', [(i, i ^ bit) for i in range(group_count)])  1.61 us
    add x1, other arithmetic, prepare(): placed(records, 0) + placed(fir_taps.reshape(1, -1), channels)  0.86 us
    pallas_call x1, Pallas kernels, lags_of(): pl.pallas_call(functools.partial(lag_kernel, row_share), out_shape=jax.Sh...  0.68 us
    convert_element_type x1, other arithmetic, prepare(): matchings.astype(jnp.float32)  0.68 us
  transfers between devices with their start and end apart: 6, of which 4 were waited for; matrix products, arithmetic and copies ran while one was open for 8% of the time, Pallas kernels for 4%

profile of v7, /device:TPU:0, one launch (start us, length us, event | category | flops | bytes accessed | tf_op | source)
XLA Modules:
  0.0 19.7 jit_solution(12033745202740305296)
XLA Ops:
  0.0 3.0 %collective-permute-start = (f32[64,256]{1,0:T(8,128)}, f32[64,256]{1,0:T(8,128)S(1)}, u32[]{:S(2)}, u32[]{:S(2)}) collective-permute-start(f32[64,256]{1,0:T(8,128)} %param.3), channel_id=1, source_target_pairs={{0,4},{4,8},{8,12},{12,0},{1,5},{5,9},{9,13},{13,1},{2,6},{6,10},{... | collective-permute-start | bytes 196616 | tf_op jit(solution)/shard_map/ppermute | solution.py:277
  3.0 2.6 %collective-permute-start.2 = (f32[64,256]{1,0:T(8,128)}, f32[64,256]{1,0:T(8,128)S(1)}, u32[]{:S(2)}, u32[]{:S(2)}) collective-permute-start(f32[64,256]{1,0:T(8,128)} %param.3), channel_id=1, source_target_pairs={{0,8},{4,12},{8,0},{12,4},{1,9},{5,13},{9,1},{13,5},{2,10},{6,14},... | collective-permute-start | bytes 196616 | tf_op jit(solution)/shard_map/ppermute | solution.py:277
  5.6 1.3 %collective-permute-start.1 = (f32[64,256]{1,0:T(8,128)}, f32[64,256]{1,0:T(8,128)S(1)}, u32[]{:S(2)}, u32[]{:S(2)}) collective-permute-start(f32[64,256]{1,0:T(8,128)} %param.3), channel_id=1, source_target_pairs={{0,12},{4,0},{8,4},{12,8},{1,13},{5,1},{9,5},{13,9},{2,14},{6,2},{... | collective-permute-start | bytes 196616 | tf_op jit(solution)/shard_map/ppermute | solution.py:277
  7.0 0.7 %convert_element_type.9 = f32[2,4]{1,0:T(2,128)S(1)} convert(s32[2,4]{1,0:T(2,128)} %param.5) | non-fusion elementwise | flops 8 | bytes 64 | tf_op jit(solution)/shard_map/convert_element_type | solution.py:76
  7.6 0.9 %pad_add_fusion.packed_ref = f32[72,256]{1,0:T(8,128)S(1)} fusion(f32[2,4]{1,0:T(2,128)S(1)} %convert_element_type.9, f32[1,129]{1,0:T(1,128)} %bitcast.4, f32[64,256]{1,0:T(8,128)} %param.3), kind=kLoop, calls=%fused_computation | loop fusion | flops 36864 | bytes 139812 | tf_op jit(solution)/shard_map/add | solution.py:74
  8.5 0.2 prepare.1
  8.7 0.0 collective-permute-done.refs_0_
  8.7 1.6 %collective-permute-done.2.refs_2_ = f32[64,256]{1,0:T(8,128)S(1)} collective-permute-done((f32[64,256]{1,0:T(8,128)}, f32[64,256]{1,0:T(8,128)S(1)}, u32[]{:S(2)}, u32[]{:S(2)}) %collective-permute-start.2) | collective-permute-done | bytes 65568 | tf_op jit(solution)/shard_map/ppermute | solution.py:277
  10.3 0.2 %collective-permute-done.1.refs_1_ = f32[64,256]{1,0:T(8,128)S(1)} collective-permute-done((f32[64,256]{1,0:T(8,128)}, f32[64,256]{1,0:T(8,128)S(1)}, u32[]{:S(2)}, u32[]{:S(2)}) %collective-permute-start.1) | collective-permute-done | bytes 65568 | tf_op jit(solution)/shard_map/ppermute | solution.py:277
  10.5 0.5 %normalize.1.normed_ref = bf16[64,1024]{1,0:T(8,128)(2,1)S(1)} custom-call(bf16[64,256]{1,0:T(8,128)(2,1)S(1)} %get-tuple-element.11.own_high, bf16[64,256]{1,0:T(8,128)(2,1)S(1)} %get-tuple-element.12.own_low, bf16[256,256]{1,0:T(8,128)(2,1)S(1)} %get-tuple-element.13.bands_ref, bf16[256,128]{1,0:T(8,128)(2,1)S(1)} %get-tuple-element.14.near_ref, ...), custom_call_target="tpu_custom_call" | custom-call | tf_op jit(solution)/shard_map/normalize/pallas_call | solution.py:147
  11.1 1.6 %collective-permute-start.4 = (bf16[64,1024]{1,0:T(8,128)(2,1)S(1)}, bf16[64,1024]{1,0:T(8,128)(2,1)S(1)}, u32[]{:S(2)}, u32[]{:S(2)}) collective-permute-start(bf16[64,1024]{1,0:T(8,128)(2,1)S(1)} %normalize.1.normed_ref), channel_id=1, source_target_pairs={{0,2},{1,3},{2,0},{3,1},{4,6},{5,7},{6,4},{7,5},{8,10},{9,11},{10,... | collective-permute-start | bytes 393224 | tf_op jit(solution)/shard_map/ppermute | solution.py:280
  12.7 0.0 collective-permute-start.3
  12.7 3.4 %collective-permute-done.4.refs_1_ = bf16[64,1024]{1,0:T(8,128)(2,1)S(1)} collective-permute-done((bf16[64,1024]{1,0:T(8,128)(2,1)S(1)}, bf16[64,1024]{1,0:T(8,128)(2,1)S(1)}, u32[]{:S(2)}, u32[]{:S(2)}) %collective-permute-start.4) | collective-permute-done | bytes 131104 | tf_op jit(solution)/shard_map/ppermute | solution.py:280
  16.1 0.0 collective-permute-start.5
  16.1 0.7 %lags.1.lagged = bf16[1040,1152]{1,0:T(8,128)(2,1)S(1)} custom-call(bf16[64,1024]{1,0:T(8,128)(2,1)S(1)} %normalize.1.normed_ref), custom_call_target="tpu_custom_call" | custom-call | flops 2097152 | bytes 4194304 | tf_op jit(solution)/shard_map/lags/pallas_call | solution.py:174
  16.8 0.0 collective-permute-done.3.refs_0_
  16.8 0.6 %collective-permute-done.5.refs_2_ = bf16[64,1024]{1,0:T(8,128)(2,1)S(1)} collective-permute-done((bf16[64,1024]{1,0:T(8,128)(2,1)S(1)}, bf16[64,1024]{1,0:T(8,128)(2,1)S(1)}, u32[]{:S(2)}, u32[]{:S(2)}) %collective-permute-start.5) | collective-permute-done | bytes 131104 | tf_op jit(solution)/shard_map/ppermute | solution.py:280
  17.5 2.2 %correlate.1 = bf16[2,16,16448]{2,1,0:T(8,128)(2,1)} custom-call(bf16[2,64,128]{2,1,0:T(8,128)(2,1)S(1)} %get-tuple-element.10.picks_ref, bf16[1040,1152]{1,0:T(8,128)(2,1)S(1)} %lags.1.lagged, bf16[64,1024]{1,0:T(8,128)(2,1)S(1)} %collective-permute-done.3.refs_0_, bf16[64,1024]{1,0:T(8,128)(2,1)S(1)} %collective-permute-done.4.refs_1_, ...), custom_call_target="tpu_custom_call" | custom-call | tf_op jit(solution)/shard_map/correlate/pallas_call | solution.py:254
Async XLA Ops:
  0.0 8.7 %collective-permute-start = (f32[64,256]{1,0:T(8,128)}, f32[64,256]{1,0:T(8,128)S(1)}, u32[]{:S(2)}, u32[]{:S(2)}) collective-permute-start(f32[64,256]{1,0:T(8,128)} %param.3), channel_id=1, source_target_pairs={{0,4},{4,8},{8,12},{12,0},{1,5},{5,9},{9,13},{13,1},{2,6},{6,10},{... | collective-permute-start | bytes 196616 | tf_op jit(solution)/shard_map/ppermute | solution.py:277
  3.0 7.3 %collective-permute-start.2 = (f32[64,256]{1,0:T(8,128)}, f32[64,256]{1,0:T(8,128)S(1)}, u32[]{:S(2)}, u32[]{:S(2)}) collective-permute-start(f32[64,256]{1,0:T(8,128)} %param.3), channel_id=1, source_target_pairs={{0,8},{4,12},{8,0},{12,4},{1,9},{5,13},{9,1},{13,5},{2,10},{6,14},... | collective-permute-start | bytes 196616 | tf_op jit(solution)/shard_map/ppermute | solution.py:277
  5.6 4.9 %collective-permute-start.1 = (f32[64,256]{1,0:T(8,128)}, f32[64,256]{1,0:T(8,128)S(1)}, u32[]{:S(2)}, u32[]{:S(2)}) collective-permute-start(f32[64,256]{1,0:T(8,128)} %param.3), channel_id=1, source_target_pairs={{0,12},{4,0},{8,4},{12,8},{1,13},{5,1},{9,5},{13,9},{2,14},{6,2},{... | collective-permute-start | bytes 196616 | tf_op jit(solution)/shard_map/ppermute | solution.py:277
  11.1 5.1 %collective-permute-start.4 = (bf16[64,1024]{1,0:T(8,128)(2,1)S(1)}, bf16[64,1024]{1,0:T(8,128)(2,1)S(1)}, u32[]{:S(2)}, u32[]{:S(2)}) collective-permute-start(bf16[64,1024]{1,0:T(8,128)(2,1)S(1)} %normalize.1.normed_ref), channel_id=1, source_target_pairs={{0,2},{1,3},{2,0},{3,1},{4,6},{5,7},{6,4},{7,5},{8,10},{9,11},{10,... | collective-permute-start | bytes 393224 | tf_op jit(solution)/shard_map/ppermute | solution.py:280
  12.7 4.1 %collective-permute-start.3 = (bf16[64,1024]{1,0:T(8,128)(2,1)S(1)}, bf16[64,1024]{1,0:T(8,128)(2,1)S(1)}, u32[]{:S(2)}, u32[]{:S(2)}) collective-permute-start(bf16[64,1024]{1,0:T(8,128)(2,1)S(1)} %normalize.1.normed_ref), channel_id=1, source_target_pairs={{0,1},{1,0},{2,3},{3,2},{4,5},{5,4},{6,7},{7,6},{8,9},{9,8},{10,11... | collective-permute-start | bytes 393224 | tf_op jit(solution)/shard_map/ppermute | solution.py:280
  16.1 1.3 %collective-permute-start.5 = (bf16[64,1024]{1,0:T(8,128)(2,1)S(1)}, bf16[64,1024]{1,0:T(8,128)(2,1)S(1)}, u32[]{:S(2)}, u32[]{:S(2)}) collective-permute-start(bf16[64,1024]{1,0:T(8,128)(2,1)S(1)} %collective-permute-done.4.refs_1_), channel_id=1, source_target_pairs={{0,1},{1,0},{2,3},{3,2},{4,5},{5,4},{6,7},{7,6},{8,9},{9,8},{10,11... | collective-permute-start | bytes 393224 | tf_op jit(solution)/shard_map/ppermute | solution.py:280

commit v8 on v7

--- a/solution.py
+++ b/solution.py
@@ -102,10 +102,11 @@
     for part in (high, low):
         part[:, :LANES] = edge
         part[:, LANES + samples :] = edge
-    for step, block in zip((0, *steps), (None, *blocks)):
-        place = lax.rem(own + (count - step), count)
+    for step, block in zip(((0, 0), *steps), (None, *blocks)):
+        back = jnp.where(lax.rem(lax.axis_index("chan"), 2) == 0, step[0], step[1])
+        place = lax.rem(own + (count - back), count)
         at = pl.ds(pl.multiple_of(LANES + place * samples_dev, LANES), samples_dev)
-        if step == 0:
+        if block is None:
             high[:, at], low[:, at] = own_high[...], own_low[...]
         else:
             high[:, at], low[:, at] = split(block[...])
@@ -273,14 +274,22 @@
     group_count = lax.axis_size("chan")
     row_share = group_ch // time_count
 
-    def turned(cells, axis, count, step):
-        return lax.ppermute(cells, axis, [(i, (i + step) % count) for i in range(count)])
+    def turned(cells, step):
+        moves = [
+            (i * group_count + g, (i + step[g % 2]) % time_count * group_count + g)
+            for i in range(time_count)
+            for g in range(group_count)
+        ]
+        return lax.ppermute(cells, ("tm", "chan"), moves)
 
     def swapped(cells, bit):
         return lax.ppermute(cells, "chan", [(i, i ^ bit) for i in range(group_count)])
 
-    steps = sorted(range(1, time_count), key=lambda step: (min(step, time_count - step), step % 2 * step))
-    blocks = [turned(records, "tm", time_count, step) for step in steps]
+    turns = range(1, time_count)
+    even = sorted(turns, key=lambda step: (min(step, time_count - step), step % 2 * step))
+    odd = sorted(turns, key=lambda step: (-min(step, time_count - step), -step))
+    steps = list(zip(even, odd))
+    blocks = [turned(records, step) for step in steps]
     *banded, own_high, own_low, slots = prepare(fir_taps, records, matchings)
     normed = normalize((own_high, own_low), banded, steps, blocks)
     if group_count == 4:

time: 19.8 us -> 19.8 us (level)
  no operation moved by 1% of the time
where the time goes in v8:
time: 19.8 us; the launch traced here: 19.6 us
  starting transfers between devices  8.58 us (43%)
  waiting for transfers between devices  5.89 us (30%)
  Pallas kernels  3.55 us (18%)
  other arithmetic  1.54 us (8%)
    ppermute x3, starting transfers between devices, turned(): return lax.ppermute(cells, ('tm', 'chan'), moves)  6.96 us
    ppermute x3, waiting for transfers between devices, swapped(): lax.ppermute(cells, 'chan', [(i, i ^ bit) for i in range(group_count)])  4.07 us
    pallas_call x1, Pallas kernels, correlate(): pl.pallas_call(functools.partial(correlate_kernel, len(groups)), out_shap...  2.19 us
    ppermute x3, waiting for transfers between devices, turned(): return lax.ppermute(cells, ('tm', 'chan'), moves)  1.82 us
    ppermute x3, starting transfers between devices, swapped(): lax.ppermute(cells, 'chan', [(i, i ^ bit) for i in range(group_count)])  1.62 us
    add x1, other arithmetic, prepare(): placed(records, 0) + placed(fir_taps.reshape(1, -1), channels)  0.86 us
    pallas_call x1, Pallas kernels, lags_of(): pl.pallas_call(functools.partial(lag_kernel, row_share), out_shape=jax.Sh...  0.68 us
    convert_element_type x1, other arithmetic, prepare(): matchings.astype(jnp.float32)  0.68 us
  transfers between devices with their start and end apart: 6, of which 4 were waited for; matrix products, arithmetic and copies ran while one was open for 8% of the time, Pallas kernels for 4%

profile of v8, /device:TPU:0, one launch (start us, length us, event | category | flops | bytes accessed | tf_op | source)
XLA Modules:
  0.0 19.6 jit_solution(17513683805281577518)
XLA Ops:
  0.0 3.0 %collective-permute-start = (f32[64,256]{1,0:T(8,128)}, f32[64,256]{1,0:T(8,128)S(1)}, u32[]{:S(2)}, u32[]{:S(2)}) collective-permute-start(f32[64,256]{1,0:T(8,128)} %param.3), channel_id=1, source_target_pairs={{0,4},{1,9},{2,6},{3,11},{4,8},{5,13},{6,10},{7,15},{8,12},{9,1},{... | collective-permute-start | bytes 196616 | tf_op jit(solution)/shard_map/ppermute | solution.py:283
  3.0 2.6 %collective-permute-start.2 = (f32[64,256]{1,0:T(8,128)}, f32[64,256]{1,0:T(8,128)S(1)}, u32[]{:S(2)}, u32[]{:S(2)}) collective-permute-start(f32[64,256]{1,0:T(8,128)} %param.3), channel_id=1, source_target_pairs={{0,8},{1,5},{2,10},{3,7},{4,12},{5,9},{6,14},{7,11},{8,0},{9,13},{... | collective-permute-start | bytes 196616 | tf_op jit(solution)/shard_map/ppermute | solution.py:283
  5.6 1.3 %collective-permute-start.1 = (f32[64,256]{1,0:T(8,128)}, f32[64,256]{1,0:T(8,128)S(1)}, u32[]{:S(2)}, u32[]{:S(2)}) collective-permute-start(f32[64,256]{1,0:T(8,128)} %param.3), channel_id=1, source_target_pairs={{0,12},{1,13},{2,14},{3,15},{4,0},{5,1},{6,2},{7,3},{8,4},{9,5},{1... | collective-permute-start | bytes 196616 | tf_op jit(solution)/shard_map/ppermute | solution.py:283
  7.0 0.7 %convert_element_type.9 = f32[2,4]{1,0:T(2,128)S(1)} convert(s32[2,4]{1,0:T(2,128)} %param.5) | non-fusion elementwise | flops 8 | bytes 64 | tf_op jit(solution)/shard_map/convert_element_type | solution.py:76
  7.6 0.9 %pad_add_fusion.packed_ref = f32[72,256]{1,0:T(8,128)S(1)} fusion(f32[2,4]{1,0:T(2,128)S(1)} %convert_element_type.9, f32[1,129]{1,0:T(1,128)} %bitcast.4, f32[64,256]{1,0:T(8,128)} %param.3), kind=kLoop, calls=%fused_computation | loop fusion | flops 36864 | bytes 139812 | tf_op jit(solution)/shard_map/add | solution.py:74
  8.5 0.2 prepare.1
  8.7 0.0 collective-permute-done.refs_0_
  8.7 1.7 %collective-permute-done.2.refs_2_ = f32[64,256]{1,0:T(8,128)S(1)} collective-permute-done((f32[64,256]{1,0:T(8,128)}, f32[64,256]{1,0:T(8,128)S(1)}, u32[]{:S(2)}, u32[]{:S(2)}) %collective-permute-start.2) | collective-permute-done | bytes 65568 | tf_op jit(solution)/shard_map/ppermute | solution.py:283
  10.3 0.2 collective-permute-done.1.refs_1_
  10.5 0.5 %normalize.1.normed_ref = bf16[64,1024]{1,0:T(8,128)(2,1)S(1)} custom-call(bf16[64,256]{1,0:T(8,128)(2,1)S(1)} %get-tuple-element.11.own_high, bf16[64,256]{1,0:T(8,128)(2,1)S(1)} %get-tuple-element.12.own_low, bf16[256,256]{1,0:T(8,128)(2,1)S(1)} %get-tuple-element.13.bands_ref, bf16[256,128]{1,0:T(8,128)(2,1)S(1)} %get-tuple-element.14.near_ref, ...), custom_call_target="tpu_custom_call" | custom-call | tf_op jit(solution)/shard_map/normalize/pallas_call | solution.py:148
  11.0 1.6 %collective-permute-start.4 = (bf16[64,1024]{1,0:T(8,128)(2,1)S(1)}, bf16[64,1024]{1,0:T(8,128)(2,1)S(1)}, u32[]{:S(2)}, u32[]{:S(2)}) collective-permute-start(bf16[64,1024]{1,0:T(8,128)(2,1)S(1)} %normalize.1.normed_ref), channel_id=1, source_target_pairs={{0,2},{1,3},{2,0},{3,1},{4,6},{5,7},{6,4},{7,5},{8,10},{9,11},{10,... | collective-permute-start | bytes 393224 | tf_op jit(solution)/shard_map/ppermute | solution.py:286
  12.6 0.0 collective-permute-start.3
  12.6 3.4 %collective-permute-done.4.refs_1_ = bf16[64,1024]{1,0:T(8,128)(2,1)S(1)} collective-permute-done((bf16[64,1024]{1,0:T(8,128)(2,1)S(1)}, bf16[64,1024]{1,0:T(8,128)(2,1)S(1)}, u32[]{:S(2)}, u32[]{:S(2)}) %collective-permute-start.4) | collective-permute-done | bytes 131104 | tf_op jit(solution)/shard_map/ppermute | solution.py:286
  16.1 0.0 collective-permute-start.5
  16.1 0.7 %lags.1.lagged = bf16[1040,1152]{1,0:T(8,128)(2,1)S(1)} custom-call(bf16[64,1024]{1,0:T(8,128)(2,1)S(1)} %normalize.1.normed_ref), custom_call_target="tpu_custom_call" | custom-call | flops 2097152 | bytes 4194304 | tf_op jit(solution)/shard_map/lags/pallas_call | solution.py:175
  16.8 0.0 collective-permute-done.3.refs_0_
  16.8 0.6 %collective-permute-done.5.refs_2_ = bf16[64,1024]{1,0:T(8,128)(2,1)S(1)} collective-permute-done((bf16[64,1024]{1,0:T(8,128)(2,1)S(1)}, bf16[64,1024]{1,0:T(8,128)(2,1)S(1)}, u32[]{:S(2)}, u32[]{:S(2)}) %collective-permute-start.5) | collective-permute-done | bytes 131104 | tf_op jit(solution)/shard_map/ppermute | solution.py:286
  17.4 2.2 %correlate.1 = bf16[2,16,16448]{2,1,0:T(8,128)(2,1)} custom-call(bf16[2,64,128]{2,1,0:T(8,128)(2,1)S(1)} %get-tuple-element.10.picks_ref, bf16[1040,1152]{1,0:T(8,128)(2,1)S(1)} %lags.1.lagged, bf16[64,1024]{1,0:T(8,128)(2,1)S(1)} %collective-permute-done.3.refs_0_, bf16[64,1024]{1,0:T(8,128)(2,1)S(1)} %collective-permute-done.4.refs_1_, ...), custom_call_target="tpu_custom_call" | custom-call | tf_op jit(solution)/shard_map/correlate/pallas_call | solution.py:255
Async XLA Ops:
  0.0 8.7 %collective-permute-start = (f32[64,256]{1,0:T(8,128)}, f32[64,256]{1,0:T(8,128)S(1)}, u32[]{:S(2)}, u32[]{:S(2)}) collective-permute-start(f32[64,256]{1,0:T(8,128)} %param.3), channel_id=1, source_target_pairs={{0,4},{1,9},{2,6},{3,11},{4,8},{5,13},{6,10},{7,15},{8,12},{9,1},{... | collective-permute-start | bytes 196616 | tf_op jit(solution)/shard_map/ppermute | solution.py:283
  3.0 7.3 %collective-permute-start.2 = (f32[64,256]{1,0:T(8,128)}, f32[64,256]{1,0:T(8,128)S(1)}, u32[]{:S(2)}, u32[]{:S(2)}) collective-permute-start(f32[64,256]{1,0:T(8,128)} %param.3), channel_id=1, source_target_pairs={{0,8},{1,5},{2,10},{3,7},{4,12},{5,9},{6,14},{7,11},{8,0},{9,13},{... | collective-permute-start | bytes 196616 | tf_op jit(solution)/shard_map/ppermute | solution.py:283
  5.6 4.9 %collective-permute-start.1 = (f32[64,256]{1,0:T(8,128)}, f32[64,256]{1,0:T(8,128)S(1)}, u32[]{:S(2)}, u32[]{:S(2)}) collective-permute-start(f32[64,256]{1,0:T(8,128)} %param.3), channel_id=1, source_target_pairs={{0,12},{1,13},{2,14},{3,15},{4,0},{5,1},{6,2},{7,3},{8,4},{9,5},{1... | collective-permute-start | bytes 196616 | tf_op jit(solution)/shard_map/ppermute | solution.py:283
  11.0 5.0 %collective-permute-start.4 = (bf16[64,1024]{1,0:T(8,128)(2,1)S(1)}, bf16[64,1024]{1,0:T(8,128)(2,1)S(1)}, u32[]{:S(2)}, u32[]{:S(2)}) collective-permute-start(bf16[64,1024]{1,0:T(8,128)(2,1)S(1)} %normalize.1.normed_ref), channel_id=1, source_target_pairs={{0,2},{1,3},{2,0},{3,1},{4,6},{5,7},{6,4},{7,5},{8,10},{9,11},{10,... | collective-permute-start | bytes 393224 | tf_op jit(solution)/shard_map/ppermute | solution.py:286
  12.6 4.1 %collective-permute-start.3 = (bf16[64,1024]{1,0:T(8,128)(2,1)S(1)}, bf16[64,1024]{1,0:T(8,128)(2,1)S(1)}, u32[]{:S(2)}, u32[]{:S(2)}) collective-permute-start(bf16[64,1024]{1,0:T(8,128)(2,1)S(1)} %normalize.1.normed_ref), channel_id=1, source_target_pairs={{0,1},{1,0},{2,3},{3,2},{4,5},{5,4},{6,7},{7,6},{8,9},{9,8},{10,11... | collective-permute-start | bytes 393224 | tf_op jit(solution)/shard_map/ppermute | solution.py:286
  16.1 1.3 %collective-permute-start.5 = (bf16[64,1024]{1,0:T(8,128)(2,1)S(1)}, bf16[64,1024]{1,0:T(8,128)(2,1)S(1)}, u32[]{:S(2)}, u32[]{:S(2)}) collective-permute-start(bf16[64,1024]{1,0:T(8,128)(2,1)S(1)} %collective-permute-done.4.refs_1_), channel_id=1, source_target_pairs={{0,1},{1,0},{2,3},{3,2},{4,5},{5,4},{6,7},{7,6},{8,9},{9,8},{10,11... | collective-permute-start | bytes 393224 | tf_op jit(solution)/shard_map/ppermute | solution.py:286
